TPU v7x, 32 devices: a whole 2x2x4 slice. The times are simulated.
32 devices in a mesh: batch: 4 (over z), seq: 8 (over y, x, core).
Axes of the slice: x: 2, y: 2, z: 4, core: 2. Of those that a mesh axis runs over, the one named last changes fastest.
Arguments:
- tokens: bfloat16 [4, 4096, 1536], P('batch', 'seq'), may hold values from -6 to 6
- norm_gain: float32 [1536], replicated, may hold values from 0.1 to 1.9
- in_weight: bfloat16 [1536, 6448], P('batch'), may hold values from -0.15625 to 0.15625
- conv_weight: float32 [4, 3328], replicated, may hold values from -3 to 3
- conv_bias: float32 [3328], replicated, may hold values from -3 to 3
- dt_bias: float32 [48], replicated, may hold values from -6 to -1
- decay_log: float32 [48], replicated, may hold values from -8 to 1
- skip_scale: float32 [48], replicated, may hold values from 0.5 to 1.5
- gate_gain: float32 [3072], replicated, may hold values from 0.1 to 1.9
- out_weight: bfloat16 [3072, 1536], P('batch'), may hold values from -0.109375 to 0.109375
- cotangent: bfloat16 [4, 4096, 1536], P('batch', 'seq'), may hold values from -6 to 6
Outputs:
- block_out: bfloat16 [4, 4096, 1536], P('batch', 'seq')
- input_grad: float32 [4, 4096, 1536], P('batch', 'seq')
- norm_gain_grad: float32 [1536], replicated
- in_weight_grad: float32 [1536, 6448], P('batch')
- conv_weight_grad: float32 [4, 3328], replicated
- conv_bias_grad: float32 [3328], replicated
- dt_bias_grad: float32 [48], replicated
- decay_log_grad: float32 [48], replicated
- skip_scale_grad: float32 [48], replicated
- gate_gain_grad: float32 [3072], replicated
- out_weight_grad: float32 [3072, 1536], P('batch')
All inputs are finite; a program needn't handle non-finite values.
Results may differ from a plain program's by a relative error of at most 0.015.
The roundings to bfloat16 on the way count: a program that leaves them out, or rounds other values in their place, can miss the bound.
Values may be sent and summed in bfloat16 or wider, within the bound.
No kernel may reach another device: no remote copies, remote signals or barrier semaphores. Data moves between devices by JAX's collectives and lax.ppermute only.
A program may use at most 320 MiB of HBM per device.

v0:
```python
import functools

import jax
import jax.numpy as jnp
from jax import lax
from jax.experimental import pallas as pl
from jax.experimental.pallas import tpu as pltpu
from jax.sharding import PartitionSpec as P

GROUP = 256
LANES = 128
HALF = GROUP // 2
HALO = 8
STEP_ROWS = 16
LOG2E = 1.4426950408889634
epsilon = 1e-05
f32 = jnp.float32
bf16 = jnp.bfloat16
MIB = 2**20


def exchange(value, axis, distance):
    count = lax.axis_size(axis)
    return lax.ppermute(value, axis, [(source, source ^ distance) for source in range(count)])


def bits_of(count):
    return [1 << k for k in range(count.bit_length() - 1)]


def placed_order(count):
    return [2 * k for k in range(count // 2)] + [2 * k + 1 for k in range(count // 2)]


def together(*values):
    return lax.optimization_barrier(values)


def far_orders():
    far = bits_of(lax.axis_size("seq"))[1:]
    return far, far[::-1]


def gather_start(value):
    half = value.shape[0] // 32 * 16
    return tuple({"base": part, "fresh": None, "near": []} for part in (value[:half], value[half:]))


def gather_stage(held, stage, late=False):
    grown = []
    for half, order in zip(held, far_orders()):
        base, fresh, near = half["base"], half["fresh"], list(half["near"])
        if stage >= 1:
            merged = base if stage == len(order) else jnp.concatenate([base, fresh], axis=0)
            if not late:
                near.append(exchange(merged if stage == 1 else fresh, "seq", 1))
            elif stage == len(order):
                near = [exchange(base, "seq", 1), exchange(fresh, "seq", 1)]
            base = merged
        if stage < len(order):
            fresh = exchange(base, "seq", order[stage])
        grown.append({"base": base, "fresh": fresh, "near": near})
    return tuple(grown)


def gather_stages():
    return len(bits_of(lax.axis_size("seq")))


def gathered(held):
    arrays, table = [], {}
    for number, (half, order) in enumerate(zip(held, far_orders())):
        indices = [0]
        for bit in order:
            indices += [index | bit for index in indices]
        middle = len(indices) // 2
        groups = [(half["base"], indices[:middle]), (half["fresh"], indices[middle:])]
        bounds = [0] + [2 << k for k in range(len(order))]
        if len(half["near"]) < len(order):
            bounds = [0, middle, len(indices)]
        for value, first, last in zip(half["near"], bounds, bounds[1:]):
            groups.append((value, [index | 1 for index in indices[first:last]]))
        for value, members in groups:
            rows = value.shape[0] // len(members)
            for turn, index in enumerate(members):
                table[number, index] = (len(arrays), turn * rows, rows)
            arrays.append(value)
    return arrays, table


def token_pieces(held):
    arrays, table = gathered(held)
    indices = range(lax.axis_size("seq"))
    return arrays, tuple(table[half, index] for index in indices for half in range(2))


def gather_all(value):
    held = gather_start(value)
    for stage in range(gather_stages()):
        held = gather_stage(held, stage)
    return held


def scatter_places(count):
    far = bits_of(count)[1:]
    table = {}
    row = {}
    for near in (1, 0):
        for sent in (True, False):
            for half, order in enumerate((far, far[::-1])):
                members = [0]
                for bit in order[:0:-1]:
                    members += [member | bit for member in members]
                for member in members:
                    index = member | near | (order[0] if sent else 0)
                    array = 0 if near else (1 + half if sent else 3)
                    table[index * 2 + half] = (array, row.get(array, 0))
                    row[array] = row.get(array, 0) + GROUP
    return tuple(table[k] for k in range(2 * count))


def scatter_shapes(count, columns):
    blocks = (count, count // 4, count // 4, count // 2)
    return [jax.ShapeDtypeStruct((part * GROUP, columns), bf16) for part in blocks]


def scatter_near(product, parts, sent):
    arriving = exchange(sent, "seq", 1)
    first, second, kept = parts
    rows = first.shape[0]

    def summed(part, row):
        return (product(part) + arriving[row : row + part.shape[0]].astype(f32)).astype(bf16)

    sends = (summed(first, 0), summed(second, rows))
    sends, kept = together(sends, kept)
    return sends, {"kept": summed(kept, 2 * rows), "arrived": ([], [])}


def scatter_rows(held, half, first, last):
    top = half * (held["kept"].shape[0] // 2)
    total = held["kept"][top + first : top + last].astype(f32)
    for value in held["arrived"][half]:
        total = total + value[first:last].astype(f32)
    return total


def scatter_far(sends, held, stage):
    orders = far_orders()
    arrived = tuple(
        [*held["arrived"][half], exchange(sends[half], "seq", orders[half][stage])]
        for half in range(2)
    )
    held = {"kept": held["kept"], "arrived": arrived}
    rows = sends[0].shape[0]
    if stage + 1 == len(orders[0]):
        return (), held
    ready = tuple(
        scatter_rows(held, half, rows // 2, rows).astype(bf16) for half in range(2)
    )
    return ready, held


def scatter_end(held):
    rows = held["arrived"][0][-1].shape[0]
    return jnp.concatenate([scatter_rows(held, half, 0, rows) for half in range(2)], axis=0)


def sum_seq(value):
    for bit in bits_of(lax.axis_size("seq")):
        value = value + exchange(value, "seq", bit)
    return value


def plane_pairs(ahead):
    planes, count = lax.axis_size("batch"), lax.axis_size("seq")
    per = count // planes
    pairs = []
    for owner in range(planes):
        for piece in range(planes):
            for k in range(per):
                holder = owner * count + piece * per + k
                user = (piece + ahead) % planes * count + owner * per + k
                pairs.append((holder, user))
    return pairs


def rows_from_owner(out_weight, width):
    per = lax.axis_size("seq") // lax.axis_size("batch")
    plane, mine = lax.axis_index("batch"), lax.axis_index("seq")
    rows = lax.dynamic_slice_in_dim(out_weight, mine % per * width, width, 0)
    return lax.psum(jnp.where(plane == mine // per, rows, jnp.zeros_like(rows)), "batch")


def to_owner(summed):
    return lax.ppermute(
        summed, ("batch", "seq"), [(user, holder) for holder, user in plane_pairs(0)]
    )


def double(held, turn):
    bits = bits_of(lax.axis_size("seq"))
    return jnp.concatenate([held, exchange(held, "seq", (bits[1:] + [1])[turn])], axis=0)


def step_values(raw):
    small = jnp.exp(-jnp.abs(raw))
    step = jnp.maximum(raw, 0.0) + jnp.log1p(small)
    sig = jnp.where(raw >= 0, 1.0, small) / (1.0 + small)
    tiny = raw < -20.0
    log_step = jnp.where(tiny, raw, jnp.log(step))
    ratio = jnp.where(tiny, 1.0, sig / step)
    return step, sig, log_step, ratio


def dot(a, b):
    return jnp.dot(a, b, preferred_element_type=f32)


def dot_nt(a, b):
    return lax.dot_general(a, b, (((1,), (1,)), ((), ())), preferred_element_type=f32)


def dot_tn(a, b):
    return lax.dot_general(a, b, (((0,), (0,)), ((), ())), preferred_element_type=f32)


def sigmoid(value):
    return 0.5 * jnp.tanh(0.5 * value) + 0.5


def silu_slope(value):
    sig = sigmoid(value)
    active = value * sig
    return active, sig + active * (1.0 - sig)


def split_parts(value, count):
    parts = []
    for _ in range(count):
        part = value.astype(bf16)
        parts.append(part)
        value = value - part.astype(f32)
    return parts


def sum_along(rows, order):
    parts = jnp.concatenate([part.astype(f32) for part in split_parts(rows, 3)], axis=0)
    total = dot(parts.astype(bf16), order)
    return total[:8] + total[8:16] + total[16:24]


def to_columns(rows):
    stacked = jnp.concatenate(rows, axis=0)
    missing = LANES - stacked.shape[0]
    return jnp.concatenate([stacked, jnp.zeros((missing, GROUP), f32)], axis=0).T


def spread_heads(value, first, heads, size):
    rows = value.shape[0]
    return jnp.concatenate(
        [jnp.broadcast_to(value[:, first + h : first + h + 1], (rows, size)) for h in range(heads)],
        axis=1,
    )


def head_ones(width, size):
    row = lax.broadcasted_iota(jnp.int32, (8, width), 0)
    column = lax.broadcasted_iota(jnp.int32, (8, width), 1)
    return (column // size == row).astype(f32).astype(bf16)


def sum_lanes(value):
    return dot_nt(jnp.ones((8, value.shape[1]), bf16), value.astype(bf16))


def ones_where(condition):
    return jnp.where(condition, 1.0, 0.0).astype(bf16)


def order_indices(length):
    row = lax.broadcasted_iota(jnp.int32, (length, length), 0)
    column = lax.broadcasted_iota(jnp.int32, (length, length), 1)
    return row, column


def fetch(arrays, table, which, target, semaphore):
    for index, (array, row, rows) in enumerate(table):

        @pl.when(which == index)
        def _():
            pltpu.make_async_copy(arrays[array].at[pl.ds(row, rows)], target, semaphore).start()


def fetched(arrays, table, buffer, semaphores, order, blocks=1):
    step = pl.program_id(0)
    slot, other = lax.rem(step, 2), lax.rem(step + 1, 2)

    def start(step, slot):
        for k in range(blocks):
            target = buffer.at[slot, pl.ds(k * GROUP, GROUP)]
            fetch(arrays, table, order(step * blocks + k), target, semaphores.at[slot])

    @pl.when(step == 0)
    def _():
        start(0, 0)

    @pl.when(step + 1 < pl.num_programs(0))
    def _():
        start(step + 1, other)

    for k in range(blocks):
        source = arrays[0].at[pl.ds(0, GROUP)]
        target = buffer.at[slot, pl.ds(k * GROUP, GROUP)]
        pltpu.make_async_copy(source, target, semaphores.at[slot]).wait()
    return buffer[slot]


def store(source, targets, table, which, semaphore):
    for index, (array, row) in enumerate(table):

        @pl.when(which == index)
        def _():
            target = targets[array].at[pl.ds(row, GROUP)]
            pltpu.make_async_copy(source, target, semaphore).start()


def stored(buffer, targets, semaphores, slot):
    target = targets[0].at[pl.ds(0, GROUP)]
    pltpu.make_async_copy(buffer.at[slot], target, semaphores.at[slot]).wait()


def in_time(place, block):
    return ((block // 2) ^ place) * 2 + block % 2


def forward_kernel(dims, table, given, place_ref, *refs):
    heads, size, states, count = dims
    width = heads * size
    conv_cols = width + 2 * states
    arrays, refs = refs[:given], refs[given:]
    w_ref, conv_w_ref, conv_b_ref, step_ref, rows_ref = refs[:5]
    conv_in_ref, active_ref, slope_ref, gate_act_ref, gate_slope_ref = refs[5:10]
    raw_ref, ssd_ref, start_ref, scaled_ref, square_ref, normed_ref = refs[10:16]
    targets = refs[16:20]
    state, padded, order, barred, buffer, semaphores, placed, out_semaphores = refs[20:]
    turn = pl.program_id(0)
    slot = lax.rem(turn, 2)

    @pl.when(turn == 0)
    def _():
        state[...] = jnp.zeros_like(state)
        padded[0:HALO] = jnp.zeros_like(padded[0:HALO])
        row, column = order_indices(GROUP)
        order[...] = ones_where(row <= column)
        row, column = order_indices(HALF)
        barred[...] = jnp.where(row >= column, 0.0, -1e30)

    @pl.when(turn >= 2)
    def _():
        stored(placed, targets, out_semaphores, slot)

    normed = fetched(
        arrays, table, buffer, semaphores, lambda step: in_time(place_ref[0], step)
    )
    normed_ref[...] = normed
    projected = dot(normed, w_ref[...])
    conv_in = projected[:, width : width + conv_cols].astype(bf16)
    conv_in_ref[...] = conv_in
    padded[HALO : HALO + GROUP] = conv_in.astype(f32)
    conv_w = conv_w_ref[...]
    taps = conv_w.shape[0]
    pre = conv_b_ref[...]
    for k in range(taps):
        top = HALO - (taps - 1) + k
        pre = pre + conv_w[k : k + 1] * padded[top : top + GROUP]
    padded[0:HALO] = padded[GROUP : GROUP + HALO]
    active, slope = silu_slope(pre)
    active = active.astype(bf16)
    active_ref[...] = active
    slope_ref[...] = slope.astype(bf16)
    signal = active[:, :width]
    entry = active[:, width : width + states]
    readout = active[:, width + states :]
    signal_wide = signal.astype(f32)

    raw = projected[:, width + conv_cols :].T[:8]
    raw_ref[0] = raw
    step, _, log_step, _ = step_values(raw + step_ref[0:8, 0:1])
    running = sum_along(step * step_ref[8:16, 0:1], order[...])
    later = running - log_step
    total = running[:, GROUP - 1 :]
    columns = to_columns([running * LOG2E, jnp.exp(running), jnp.exp(total - later)])
    later = later * LOG2E
    early_wide = spread_heads(columns, 8, heads, size)
    tail_wide = spread_heads(columns, 16, heads, size)
    first, second = slice(0, HALF), slice(HALF, GROUP)
    scores = dot_nt(readout[first], entry[first])
    later_scores = dot_nt(readout[second], entry)
    within = []
    for h in range(heads):
        part = signal[:, h * size : (h + 1) * size]
        begin, end = columns[first, h : h + 1], columns[second, h : h + 1]
        row_first, row_second = later[h : h + 1, first], later[h : h + 1, second]
        near = jnp.exp2(begin - row_first + barred[...]) * scores
        full = jnp.exp2(end - row_first) * later_scores[:, first]
        last = jnp.exp2(end - row_second + barred[...]) * later_scores[:, second]
        both = jnp.concatenate([full.astype(bf16), last.astype(bf16)], axis=1)
        within.append(
            jnp.concatenate([dot(near.astype(bf16), part[first]), dot(both, part)], axis=0)
        )
    start = state[...]
    start_low = start.astype(bf16)
    start_ref[0] = start_low
    carried = dot(readout, start_low) * early_wide
    ssd = jnp.concatenate(within, axis=1) + carried + rows_ref[0:1] * signal_wide
    tail = (signal_wide * tail_wide).astype(bf16)
    state[...] = start * early_wide[GROUP - 1 :] + dot_tn(entry, tail)

    gate_act, gate_slope = silu_slope(projected[:, :width])
    gate_act_ref[...] = gate_act.astype(bf16)
    gate_slope_ref[...] = gate_slope.astype(bf16)
    ssd_ref[...] = ssd
    gated = ssd * gate_act
    scaled = (gated * rows_ref[1:2]).astype(bf16)
    scaled_ref[...] = scaled
    square_ref[0] = sum_lanes(gated * gated)
    placed[slot] = scaled
    where = in_time(place_ref[0], turn)
    store(placed.at[slot], targets, scatter_places(count), where, out_semaphores.at[slot])

    @pl.when(turn == pl.num_programs(0) - 1)
    def _():
        for other in range(2):
            stored(placed, targets, out_semaphores, other)


def time_estimate(microseconds, accessed):
    return pl.CostEstimate(
        flops=int(microseconds * 1.1e9), bytes_accessed=int(accessed), transcendentals=0
    )


def fixed(shape):
    return pl.BlockSpec(shape, lambda turn, place: (0,) * len(shape), pipeline_mode=pl.Buffered(1))


def anywhere(values):
    return [pl.BlockSpec(memory_space=pltpu.HBM)] * len(values)


def run_forward(place, pieces, params, dims):
    heads, size, states, count = dims
    arrays, table = pieces
    dim = params[0].shape[0]
    width, conv_cols = heads * size, params[1].shape[1]
    blocks = len(table)
    tokens = blocks * GROUP

    def moving(columns):
        return pl.BlockSpec((GROUP, columns), lambda turn, place: (turn, 0))

    def rows_of_block(height, columns):
        return pl.BlockSpec((1, height, columns), lambda turn, place: (turn, 0, 0))

    results = pl.pallas_call(
        functools.partial(forward_kernel, dims, table, len(arrays)),
        grid_spec=pltpu.PrefetchScalarGridSpec(
            num_scalar_prefetch=1,
            grid=(blocks,),
            in_specs=[*anywhere(arrays), *[fixed(param.shape) for param in params]],
            out_specs=[
                moving(conv_cols),
                moving(conv_cols),
                moving(conv_cols),
                moving(width),
                moving(width),
                rows_of_block(8, GROUP),
                moving(width),
                rows_of_block(states, width),
                moving(width),
                rows_of_block(8, GROUP),
                moving(dim),
                *anywhere(range(4)),
            ],
            scratch_shapes=[
                pltpu.VMEM((states, width), f32),
                pltpu.VMEM((HALO + GROUP, conv_cols), f32),
                pltpu.VMEM((GROUP, GROUP), bf16),
                pltpu.VMEM((HALF, HALF), f32),
                pltpu.VMEM((2, GROUP, dim), bf16),
                pltpu.SemaphoreType.DMA((2,)),
                pltpu.VMEM((2, GROUP, width), bf16),
                pltpu.SemaphoreType.DMA((2,)),
            ],
        ),
        out_shape=[
            jax.ShapeDtypeStruct((tokens, conv_cols), bf16),
            jax.ShapeDtypeStruct((tokens, conv_cols), bf16),
            jax.ShapeDtypeStruct((tokens, conv_cols), bf16),
            jax.ShapeDtypeStruct((tokens, width), bf16),
            jax.ShapeDtypeStruct((tokens, width), bf16),
            jax.ShapeDtypeStruct((blocks, 8, GROUP), f32),
            jax.ShapeDtypeStruct((tokens, width), f32),
            jax.ShapeDtypeStruct((blocks, states, width), bf16),
            jax.ShapeDtypeStruct((tokens, width), bf16),
            jax.ShapeDtypeStruct((blocks, 8, GROUP), f32),
            jax.ShapeDtypeStruct((tokens, dim), bf16),
            *scatter_shapes(count, width),
        ],
        compiler_params=pltpu.CompilerParams(vmem_limit_bytes=60 * MIB),
        cost_estimate=time_estimate(blocks * 3.0, tokens * (4 * dim + 24 * width)),
        name="forward_blocks",
    )(place, *arrays, *params)
    return results[:11], results[11:]


def out_grad_kernel(table, given, place_ref, *refs):
    arrays, refs = refs[:given], refs[given:]
    scaled_ref, out_rows_ref, out_grad_ref, slope_ref, cot_ref = refs[:5]
    buffer, semaphores, copied = refs[5:]
    place, turn = place_ref[0], pl.program_id(0)
    rows = buffer.shape[1]

    def copy_on(turn):
        target = cot_ref.at[pl.ds(pl.multiple_of(turn * rows, rows), rows)]
        return pltpu.make_async_copy(buffer.at[lax.rem(turn, 2)], target, copied)

    @pl.when(turn >= 1)
    def _():
        copy_on(turn - 1).wait()

    cot = fetched(arrays, table, buffer, semaphores, lambda block: in_time(place, block), 2)
    copy_on(turn).start()
    out_grad = dot_nt(cot, out_rows_ref[...])
    out_grad_ref[...] = out_grad
    for block in range(2):
        here = slice(block * GROUP, (block + 1) * GROUP)
        slope_ref[block] = sum_lanes(out_grad[here] * scaled_ref[here].astype(f32))

    @pl.when(turn == pl.num_programs(0) - 1)
    def _():
        copy_on(turn).wait()


def run_out_grad(place, cots, scaled, out_rows):
    arrays, table = cots
    width, dim = out_rows.shape
    blocks = len(table)
    tokens = blocks * GROUP
    return pl.pallas_call(
        functools.partial(out_grad_kernel, table, len(arrays)),
        grid_spec=pltpu.PrefetchScalarGridSpec(
            num_scalar_prefetch=1,
            grid=(blocks // 2,),
            in_specs=[
                *anywhere(arrays),
                pl.BlockSpec((2 * GROUP, width), lambda turn, place: (turn, 0)),
                fixed(out_rows.shape),
            ],
            out_specs=[
                pl.BlockSpec((2 * GROUP, width), lambda turn, place: (turn, 0)),
                pl.BlockSpec((2, 8, GROUP), lambda turn, place: (turn, 0, 0)),
                *anywhere(range(1)),
            ],
            scratch_shapes=[
                pltpu.VMEM((2, 2 * GROUP, dim), bf16),
                pltpu.SemaphoreType.DMA((2,)),
                pltpu.SemaphoreType.DMA,
            ],
        ),
        out_shape=[
            jax.ShapeDtypeStruct((tokens, width), f32),
            jax.ShapeDtypeStruct((blocks, 8, GROUP), f32),
            jax.ShapeDtypeStruct((tokens, dim), bf16),
        ],
        compiler_params=pltpu.CompilerParams(vmem_limit_bytes=60 * MIB),
        cost_estimate=time_estimate(12, tokens * (4 * dim + 6 * width)),
        name="out_grad",
    )(place, *arrays, scaled, out_rows)


def backward_kernel(dims, place_ref, *refs):
    heads, size, states, count = dims
    width = heads * size
    conv_cols = width + 2 * states
    conv_in_ref, active_ref, slope_ref, gate_act_ref, gate_slope_ref = refs[:5]
    raw_ref, ssd_ref, start_ref, out_grad_ref, norm_ref = refs[5:10]
    conv_w_ref, step_ref, rows_ref = refs[10:13]
    out_ref, targets = refs[13], refs[14:18]
    sums = refs[18:24]
    gain_ref, skip_ref, conv_wg_ref, conv_bg_ref, bias_ref, rate_ref = sums
    state, pre_grads, order, back_order, barred, placed, semaphores = refs[24:]
    taps = conv_w_ref.shape[0]
    turn = pl.program_id(0)
    slot = lax.rem(turn, 2)

    @pl.when(turn >= 2)
    def _():
        stored(placed, targets, semaphores, slot)

    @pl.when(pl.program_id(0) == 0)
    def _():
        state[...] = jnp.zeros_like(state)
        pre_grads[0:HALO] = jnp.zeros_like(pre_grads[0:HALO])
        for total in sums:
            total[...] = jnp.zeros_like(total)
        row, column = order_indices(GROUP)
        order[...] = ones_where(row <= column)
        back_order[...] = ones_where(row >= column)
        row, column = order_indices(HALF)
        barred[...] = jnp.where(row <= column, 0.0, -1e30)

    gate_act, ssd, out_grad = gate_act_ref[...].astype(f32), ssd_ref[...], out_grad_ref[...]
    norms = norm_ref[0].T
    scale, slope = norms[:, 0:1], norms[:, 1:2]
    gated = ssd * gate_act
    gain_ref[...] += jnp.sum(out_grad * (gated * scale), axis=0, keepdims=True)
    gated_grad = out_grad * (rows_ref[1:2] * scale) - gated * slope
    grad_low = (gated_grad * gate_act).astype(bf16)
    gate_grad = (gated_grad * ssd * gate_slope_ref[...].astype(f32)).astype(bf16)
    out_ref[:, :width] = gate_grad
    placed[slot, :, :width] = gate_grad
    ssd_grad = grad_low.astype(f32)

    raw = raw_ref[0] + step_ref[0:8, 0:1]
    rate = step_ref[8:16, 0:1]
    step, sig, log_step, ratio = step_values(raw)
    decay = step * rate
    running = sum_along(decay, order[...])
    later = running - log_step
    total = running[:, GROUP - 1 :]
    columns = to_columns([later * LOG2E, jnp.exp(running), jnp.exp(total - later)])
    running = running * LOG2E
    early_wide = spread_heads(columns, 8, heads, size)
    tail_wide = spread_heads(columns, 16, heads, size)

    signal = active_ref[:, :width]
    entry = active_ref[:, width : width + states]
    readout = active_ref[:, width + states :]
    signal_wide = signal.astype(f32)
    start_low = start_ref[0]
    end_grad = state[...]
    end_low = end_grad.astype(bf16)
    first, second = slice(0, HALF), slice(HALF, GROUP)
    scores = dot_nt(entry[first], readout)
    later_scores = dot_nt(entry[second], readout[second])
    near_grad, far_grad, last_grad = 0.0, 0.0, 0.0
    within = []
    for h in range(heads):
        part, grad = signal[:, h * size : (h + 1) * size], grad_low[:, h * size : (h + 1) * size]
        begin, end = columns[first, h : h + 1], columns[second, h : h + 1]
        row_first, row_second = running[h : h + 1, first], running[h : h + 1, second]
        near = jnp.exp2(row_first - begin + barred[...])
        full = jnp.exp2(row_second - begin)
        last = jnp.exp2(row_second - end + barred[...])
        both = jnp.concatenate(
            [
                (near * scores[:, first]).astype(bf16),
                (full * scores[:, second]).astype(bf16),
            ],
            axis=1,
        )
        final = (last * later_scores).astype(bf16)
        within.append(jnp.concatenate([dot(both, grad), dot(final, grad[second])], axis=0))
        cross = dot_nt(part[first], grad)
        near_grad = near_grad + cross[:, first] * near
        far_grad = far_grad + cross[:, second] * full
        last_grad = last_grad + dot_nt(part[second], grad[second]) * last
    tail_grad = tail_wide * dot(entry, end_low)
    signal_grad = jnp.concatenate(within, axis=1) + tail_grad
    score_first = jnp.concatenate([near_grad, far_grad], axis=1).astype(bf16)
    score_second = last_grad.astype(bf16)
    tail = (signal_wide * tail_wide).astype(bf16)
    head_grad = (ssd_grad * early_wide).astype(bf16)
    entry_grad = jnp.concatenate(
        [dot(score_first, readout), dot(score_second, readout[second])], axis=0
    ) + dot_nt(tail, end_low)
    readout_grad = dot_tn(score_first, entry[first]) + dot_nt(head_grad, start_low)
    readout_last = readout_grad[second] + dot_tn(score_second, entry[second])
    total_wide = early_wide[GROUP - 1 :]
    state[...] = end_grad * total_wide + dot_tn(readout, head_grad)

    skip = rows_ref[0:1]
    ones = head_ones(width, size)
    column_part = signal_wide * signal_grad
    row_part = ssd_grad * (ssd - skip * signal_wide)
    end_part = jnp.sum(signal_wide * tail_grad, axis=0, keepdims=True) + total_wide * jnp.sum(
        start_low.astype(f32) * end_grad, axis=0, keepdims=True
    )

    def head_sums(value, parts):
        return sum(dot_nt(ones, part) for part in split_parts(value, parts))

    end_rows = head_sums(jnp.broadcast_to(end_part, (8, width)), 2)[:, 0:1]
    decay_grad = sum_along(head_sums(row_part - column_part, 2), back_order[...]) + end_rows
    raw_grad = head_sums(column_part, 1) * ratio + decay_grad * rate * sig
    skip_ref[...] += jnp.sum(ssd_grad * signal_wide, axis=0, keepdims=True)
    bias_ref[...] += raw_grad
    rate_ref[...] += decay_grad * decay
    raw_low = to_columns([raw_grad]).astype(bf16)
    out_ref[:, width + conv_cols :] = raw_low
    placed[slot, :, width + conv_cols :] = raw_low

    pre_grads[GROUP : GROUP + HALO] = pre_grads[0:HALO]
    pre_grads[0:GROUP, :width] = (signal_grad + skip * ssd_grad) * slope_ref[:, :width].astype(f32)
    sides = slope_ref[:, width:].astype(f32)
    pre_grads[0:GROUP, width : width + states] = entry_grad * sides[:, :states]
    pre_grads[0:HALF, width + states :] = readout_grad[first] * sides[first, states:]
    pre_grads[HALF:GROUP, width + states :] = readout_last * sides[second, states:]
    conv_w = conv_w_ref[...]
    conv_in = conv_in_ref[...].astype(f32)
    conv_grad = 0.0
    for k in range(taps):
        ahead = taps - 1 - k
        shifted = pre_grads[ahead : ahead + GROUP]
        conv_grad = conv_grad + conv_w[k : k + 1] * shifted
        conv_wg_ref[k : k + 1] += jnp.sum(shifted * conv_in, axis=0, keepdims=True)
        if ahead == 0:
            conv_bg_ref[...] += jnp.sum(shifted, axis=0, keepdims=True)
    conv_low = conv_grad.astype(bf16)
    out_ref[:, width : width + conv_cols] = conv_low
    placed[slot, :, width : width + conv_cols] = conv_low

    where = in_time(place_ref[0], pl.num_programs(0) - 1 - turn)
    store(placed.at[slot], targets, scatter_places(count), where, semaphores.at[slot])

    @pl.when(turn == pl.num_programs(0) - 1)
    def _():
        for other in range(2):
            stored(placed, targets, semaphores, other)


def run_backward(place, values, params, dims):
    heads, size, states, count = dims
    conv_cols, width = values[0].shape[1], heads * size
    tokens = values[0].shape[0]
    blocks = tokens // GROUP
    last = blocks - 1
    out_cols = width + conv_cols + LANES

    def moving(columns):
        return pl.BlockSpec((GROUP, columns), lambda turn, place: (last - turn, 0))

    def rows_of_block():
        return pl.BlockSpec((1, 8, GROUP), lambda turn, place: (last - turn, 0, 0))

    sums = [(1, width), (1, width), params[0].shape, (1, conv_cols), (8, GROUP), (8, GROUP)]
    return pl.pallas_call(
        functools.partial(backward_kernel, dims),
        grid_spec=pltpu.PrefetchScalarGridSpec(
            num_scalar_prefetch=1,
            grid=(blocks,),
            in_specs=[
                moving(conv_cols),
                moving(conv_cols),
                moving(conv_cols),
                moving(width),
                moving(width),
                rows_of_block(),
                moving(width),
                pl.BlockSpec((1, states, width), lambda turn, place: (last - turn, 0, 0)),
                moving(width),
                rows_of_block(),
                *[fixed(param.shape) for param in params],
            ],
            out_specs=[
                moving(out_cols),
                *anywhere(range(4)),
                *[fixed(shape) for shape in sums],
            ],
            scratch_shapes=[
                pltpu.VMEM((states, width), f32),
                pltpu.VMEM((GROUP + HALO, conv_cols), f32),
                pltpu.VMEM((GROUP, GROUP), bf16),
                pltpu.VMEM((GROUP, GROUP), bf16),
                pltpu.VMEM((HALF, HALF), f32),
                pltpu.VMEM((2, GROUP, out_cols), bf16),
                pltpu.SemaphoreType.DMA((2,)),
            ],
        ),
        out_shape=[
            jax.ShapeDtypeStruct((tokens, out_cols), bf16),
            *scatter_shapes(count, out_cols),
        ]
        + [jax.ShapeDtypeStruct(shape, f32) for shape in sums],
        compiler_params=pltpu.CompilerParams(vmem_limit_bytes=60 * MIB),
        cost_estimate=time_estimate(blocks * 3.5, tokens * 40 * width),
        name="backward_blocks",
    )(place, *values, *params)


def widen_kernel(place_ref, piece_ref, out_ref):
    out_ref[...] = piece_ref[0].astype(f32)


def assemble_out(place, pieces, per):
    count, size, dim = pieces.shape
    groups = count // per

    def source(turn, place):
        relative = (turn % groups * per + turn // groups) ^ place[0]
        return ((relative & 1) * (count // 2) + (relative >> 1), 0, 0)

    return pl.pallas_call(
        widen_kernel,
        grid_spec=pltpu.PrefetchScalarGridSpec(
            num_scalar_prefetch=1,
            grid=(count,),
            in_specs=[pl.BlockSpec((1, size, dim), source)],
            out_specs=pl.BlockSpec((size, dim), lambda turn, place: (turn, 0)),
        ),
        out_shape=jax.ShapeDtypeStruct((count * size, dim), f32),
        cost_estimate=time_estimate(5, count * size * dim * 6),
        name="assemble_out_weight_grad",
    )(place, pieces)


def assemble_kernel(dims, pieces_ref, out_ref):
    heads, size, states, count = dims
    width, shared = heads * size, 2 * states
    inner = count * width
    total = 0.0
    for device in range(count):
        columns = pieces_ref[device].astype(f32).T
        out_ref[device * width : (device + 1) * width] = columns[:width]
        out_ref[inner + device * width : inner + (device + 1) * width] = columns[width : 2 * width]
        total = total + columns[2 * width : 2 * width + shared]
        last = 2 * inner + shared + device * heads
        out_ref[last : last + heads] = columns[2 * width + shared : 2 * width + shared + heads]
    out_ref[2 * inner : 2 * inner + shared] = total


def assemble(pieces, dims):
    heads, size, states, count = dims
    _, rows, columns = pieces.shape
    tile = LANES if rows % LANES == 0 else rows
    out_rows = 2 * count * heads * size + 2 * states + count * heads
    return pl.pallas_call(
        functools.partial(assemble_kernel, dims),
        grid=(rows // tile,),
        in_specs=[pl.BlockSpec((count, tile, columns), lambda turn: (0, turn, 0))],
        out_specs=pl.BlockSpec((out_rows, tile), lambda turn: (0, turn)),
        out_shape=jax.ShapeDtypeStruct((out_rows, rows), f32),
        compiler_params=pltpu.CompilerParams(vmem_limit_bytes=60 * MIB),
        cost_estimate=time_estimate(8, out_rows * rows * 6),
        name="assemble_in_weight_grad",
    )(pieces)


def body(
    tokens,
    norm_gain,
    in_weight,
    conv_weight,
    conv_bias,
    dt_bias,
    decay_log,
    skip_scale,
    gate_gain,
    out_weight,
    cotangent,
):
    count, mine = lax.axis_size("seq"), lax.axis_index("seq")
    place = mine.astype(jnp.int32).reshape(1)
    inner, all_heads, conv_all = gate_gain.shape[0], dt_bias.shape[0], conv_bias.shape[0]
    size, states = inner // all_heads, (conv_all - inner) // 2
    heads, width = all_heads // count, inner // count
    dims = (heads, size, states, count)
    shared = 2 * states
    conv_cols = width + shared
    tok_rows = tokens.shape[1]
    per_plane = out_weight.shape[0] // width

    def own(vector, per, first=0):
        return lax.dynamic_slice_in_dim(vector, first + mine * per, per, vector.ndim - 1)

    def own_conv(array, first=0):
        return jnp.concatenate(
            [own(array, width, first), array[..., first + inner : first + conv_all]], axis=-1
        )

    tokens_row = tokens[0].astype(f32)
    inverse = lax.rsqrt(jnp.mean(tokens_row * tokens_row, axis=-1, keepdims=True) + epsilon)
    normed_own = (tokens_row * inverse * norm_gain).astype(bf16)
    step_own = own(in_weight, heads, inner + conv_all)
    w_own = jnp.concatenate(
        [
            own(in_weight, width),
            own_conv(in_weight, inner),
            jnp.pad(step_own, ((0, 0), (0, LANES - heads))),
        ],
        axis=1,
    )
    w_cols = lax.all_gather(w_own, "batch", axis=0, tiled=True)
    stages = gather_stages()
    held = gather_stage(gather_stage(gather_start(normed_own), 0), 1)
    held, cots = together(held, gather_start(cotangent[0]))
    cots = gather_stage(cots, 0)
    for stage in range(2, stages):
        held = gather_stage(held, stage)
    w_cols, held, cots, out_owned = together(w_cols, held, cots, out_weight)
    cots = gather_stage(cots, 1)
    out_rows = rows_from_owner(out_owned, width)

    conv_w, conv_b = own_conv(conv_weight), own_conv(conv_bias)[None]
    per_head = jnp.stack([own(dt_bias, heads), -jnp.exp(own(decay_log, heads))])
    per_head = jnp.pad(per_head, ((0, 0), (0, 8 - heads))).reshape(16, 1)
    step_rows = jnp.broadcast_to(per_head, (16, LANES))
    gain_own = own(gate_gain, width)[None]
    rows = jnp.concatenate(
        [jnp.repeat(own(skip_scale, heads), size)[None], gain_own, jnp.zeros((6, width), f32)],
        axis=0,
    )
    results, out_parts = run_forward(
        place, token_pieces(held), (w_cols, conv_w, conv_b, step_rows, rows), dims
    )
    conv_in, active, slope, gate_act, gate_slope, raw, ssd, starts, scaled, squares, normed = results
    out_parts, cots, out_rows = together(out_parts, cots, out_rows)
    for stage in range(2, stages):
        cots = gather_stage(cots, stage)

    def out_product(part):
        return dot(part, out_rows)

    out_send = out_product(out_parts[0]).astype(bf16)
    out_send, cots = together(out_send, cots)
    out_grad, slopes, cot = run_out_grad(place, token_pieces(cots), scaled, out_rows)
    sums = jnp.stack([squares[:, 0].reshape(-1), slopes[:, 0].reshape(-1)])
    out_ready, out_held = scatter_near(out_product, out_parts[1:], out_send)
    sums = sums + exchange(sums, "seq", 1)
    sums, first = together(sums, out_ready[0])
    sums = sums + exchange(sums, "seq", 2)
    sums, second = together(sums, out_ready[1])
    for bit in bits_of(count)[2:]:
        sums = sums + exchange(sums, "seq", bit)
    scale = lax.rsqrt(sums[0] / inner + epsilon)
    norms = jnp.stack([scale, scale * scale * scale * sums[1] / inner])
    norms = jnp.pad(norms, ((0, 6), (0, 0))).reshape(8, -1, GROUP).swapaxes(0, 1)
    normed_out = (scaled.astype(f32) * scale[:, None]).astype(bf16)
    out_term = jnp.einsum("te,td->ed", normed_out, cot, preferred_element_type=f32)
    out_term, norms, first, second = together(out_term.astype(bf16), norms, first, second)
    out_sum = lax.psum_scatter(out_term, "batch", scatter_dimension=0, tiled=True)
    out_ready, out_held = scatter_far((first, second), out_held, 0)

    values = (conv_in, active, slope, gate_act, gate_slope, raw, ssd, starts, out_grad, norms)
    results = run_backward(place, values, (conv_w, step_rows, rows), dims)
    proj_grad, back_parts = results[0], results[1:5]
    proj_grad, back_parts, out_ready, out_held, out_sum = together(
        proj_grad, back_parts, out_ready, out_held, out_sum
    )

    def back_product(part):
        return jnp.einsum("tf,df->td", part, w_cols, preferred_element_type=f32)

    def weight_product(part):
        return jnp.einsum("td,tf->df", normed, part, preferred_element_type=f32).astype(bf16)

    for stage in range(1, stages - 1):
        out_ready, out_held = scatter_far(out_ready, out_held, stage)
    back_send = back_product(back_parts[0]).astype(bf16)
    back_send, proj_grad = together(back_send, proj_grad)
    in_term = weight_product(proj_grad)
    in_term, keeps, out_held = together(in_term, back_parts[1:], out_held)
    in_sum = lax.psum_scatter(in_term, "batch", scatter_dimension=0, tiled=True)
    back_ready, back_held = scatter_near(back_product, keeps, back_send)
    back_ready, out_sum = together(back_ready, out_sum)
    back_ready, back_held = scatter_far(back_ready, back_held, 0)
    out_pieces = to_owner(out_sum)[None]

    back_held["kept"], in_term, results = together(back_held["kept"], in_term, results[5:])
    gain_term, skip_term, conv_w_term, conv_b_term, bias_term, rate_term = results
    norm_gain_term = jnp.sum(in_term.astype(f32) * w_cols.astype(f32), axis=1) / norm_gain

    def among_heads(vector, per, total):
        return lax.dynamic_update_slice_in_dim(jnp.zeros((total,), f32), vector, mine * per, 0)

    def among_conv(array):
        wide = jnp.zeros((array.shape[0], inner), f32)
        wide = lax.dynamic_update_slice_in_dim(wide, array[:, :width], mine * width, 1)
        return jnp.concatenate([wide, array[:, width:]], axis=1).reshape(-1)

    skip_heads = jnp.sum(skip_term.reshape(heads, size), axis=1)
    terms = [
        norm_gain_term,
        among_conv(conv_w_term),
        among_conv(conv_b_term),
        among_heads(jnp.sum(bias_term[:heads], axis=1), heads, all_heads),
        among_heads(jnp.sum(rate_term[:heads], axis=1), heads, all_heads),
        among_heads(skip_heads, heads, all_heads),
        among_heads(gain_term[0], width, inner),
    ]
    vector = jnp.concatenate(terms)
    padding = -vector.shape[0] % (8 * LANES)
    vector = jnp.pad(vector, (0, padding)).reshape(-1, LANES)

    axes = [(axis, bit) for axis in ("seq", "batch") for bit in bits_of(lax.axis_size(axis))]
    vector = vector + exchange(vector, *axes.pop(0))
    back_ready, vector, out_pieces = together(back_ready, vector, out_pieces)
    for stage in range(1, stages - 1):
        back_ready, back_held = scatter_far(back_ready, back_held, stage)
    out_pieces = double(out_pieces, 0)
    vector = vector + exchange(vector, *axes.pop(0))
    back_held["arrived"], vector, out_pieces, in_sum = together(
        back_held["arrived"], vector, out_pieces, in_sum
    )
    pieces = lax.all_gather(in_sum, "seq", axis=0, tiled=False)
    in_weight_grad = assemble(pieces, dims).T
    for stage in range(1, stages):
        out_pieces = double(out_pieces, stage)
    while axes:
        vector = vector + exchange(vector, *axes.pop(0))
    vector = vector.reshape(-1)
    normed_grad = scatter_end(back_held)
    cot_row = cotangent[0].astype(f32)
    gained = norm_gain * normed_grad
    slope = inverse * inverse * inverse * jnp.mean(gained * tokens_row, axis=-1, keepdims=True)
    input_grad = cot_row + inverse * gained - tokens_row * slope
    own_scale = lax.dynamic_slice_in_dim(scale, mine * tok_rows, tok_rows, 0)[:, None]
    block_out = (tokens_row + own_scale * scatter_end(out_held)).astype(bf16)
    out_weight_grad = assemble_out(place, out_pieces, per_plane)

    parts, offset = [], 0
    for term in terms:
        parts.append(vector[offset : offset + term.shape[0]])
        offset += term.shape[0]
    return (
        block_out[None],
        input_grad[None],
        parts[0],
        in_weight_grad,
        parts[1].reshape(conv_weight.shape),
        parts[2],
        parts[3],
        parts[4],
        parts[5],
        parts[6],
        out_weight_grad,
    )


def solution(mesh):
    placed = (
        P("batch", "seq", None),
        P(),
        P("batch", None),
        P(),
        P(),
        P(),
        P(),
        P(),
        P(),
        P("batch", None),
        P("batch", "seq", None),
    )
    return jax.shard_map(
        body,
        mesh=mesh,
        in_specs=placed,
        out_specs=(
            P("batch", "seq", None),
            P("batch", "seq", None),
            P(),
            P("batch", None),
            P(),
            P(),
            P(),
            P(),
            P(),
            P(),
            P("batch", None),
        ),
        check_vma=False,
    )
```

profile of v0, /device:TPU:0, one launch (start us, length us, event | category | flops | bytes accessed | tf_op | source)
XLA Modules:
  0.0 491.0 jit_solution(960702055454469087)
XLA Ops:
  7.2 1.0 slice.151
  9.2 1.1 constant_dynamic-slice_fusion.4
  10.8 1.0 fusion.19
  14.3 3.0 collective-permute-start
  17.3 1.5 collective-permute-start.3
  18.9 16.0 %collective-permute-done = bf16[256,1536]{1,0:T(8,128)(2,1)S(1)} collective-permute-done((bf16[256,1536]{1,0:T(8,128)(2,1)S(1)}, bf16[256,1536]{1,0:T(8,128)(2,1)S(1)}, u32[]{:S(2)}, u32[]{:S(2)}) %collective-permute-start) | collective-permute-done | bytes 786464 | tf_op jit(solution)/shard_map/ppermute | solution.py:24
  35.1 1.8 collective-permute-start.1
  37.4 1.5 collective-permute-start.4
  39.0 33.0 %collective-permute-done.1.refs_1_ = bf16[512,1536]{1,0:T(8,128)(2,1)} collective-permute-done((bf16[512,1536]{1,0:T(8,128)(2,1)S(1)}, bf16[512,1536]{1,0:T(8,128)(2,1)}, u32[]{:S(2)}, u32[]{:S(2)}) %collective-permute-start.1) | collective-permute-done | bytes 1572896 | tf_op jit(solution)/shard_map/ppermute | solution.py:24
  72.0 2.1 collective-permute-done.4.refs_5_
  74.6 1.5 collective-permute-start.8
  80.2 13.9 %collective-permute-done.8 = bf16[256,1536]{1,0:T(8,128)(2,1)S(1)} collective-permute-done((bf16[256,1536]{1,0:T(8,128)(2,1)S(1)}, bf16[256,1536]{1,0:T(8,128)(2,1)S(1)}, u32[]{:S(2)}, u32[]{:S(2)}) %collective-permute-start.8) | collective-permute-done | bytes 786464 | tf_op jit(solution)/shard_map/ppermute | solution.py:24
  94.1 1.2 collective-permute-done.9
  95.3 1.0 constant_dynamic-update-slice_fusion.3
  96.3 1.0 constant_dynamic-update-slice_fusion.2.refs_4_
  97.8 0.9 constant_dynamic-update-slice_fusion.1
  98.7 0.9 constant_dynamic-update-slice_fusion.refs_0_
  99.9 0.9 collective-permute-start.10
  100.9 1.3 dynamic-slice_select_fusion
  102.9 58.1 %forward_blocks.1 = (bf16[4096,640]{1,0:T(8,128)(2,1)}, bf16[4096,640]{1,0:T(8,128)(2,1)}, bf16[4096,640]{1,0:T(8,128)(2,1)}, bf16[4096,384]{1,0:T(8,128)(2,1)},...) custom-call(s32[1]{0:T(128)} %bitcast.place_ref, ...), custom_call_target="tpu_custom_call" | custom-call | flops 52800000000 | bytes 62914560 | tf_op jit(solution)/shard_map/forward_blocks/pallas_call | solution.py:466
  161.7 8.4 %convolution_convert_fusion.2 = bf16[2048,1536]{1,0:T(8,128)(2,1)} fusion(bf16[2048,384]{1,0:T(8,128)(2,1)} %get-tuple-element.167, bf16[384,1536]{1,0:T(8,128)(2,1)} %all-reduce.6.cloned.1.call-done.refs_9_), kind=kOutput, calls=%fused_computation.2 | convolution fusion | flops 2419064832 | bytes 9043968 | tf_op jit(solution)/shard_map/dot_general | solution.py:217
  170.2 1.1 copy-done.33
  172.7 18.4 %out_grad.1 = (f32[4096,384]{1,0:T(8,128)}, f32[16,8,256]{2,1,0:T(8,128)}, bf16[4096,1536]{1,0:T(8,128)(2,1)}) custom-call(s32[1]{0:T(128)} %bitcast.place_ref, bf16[512,1536]{1,0:T(8,128)(2,1)} %constant_dynamic-update-slice_fusion.refs_0_, bf16[512,1536]{1,0:T(8,128)(2,1)} %copy-done.32, bf16[512,1536]{1,0:T(8,128)(2,1)} %copy-done.31, ...), custom_call_target="tpu_custom_call" | custom-call | flops 13200000000 | bytes 34603008 | tf_op jit(solution)/shard_map/out_grad/pallas_call | solution.py:551
  191.1 0.9 slice.161
  192.1 1.2 collective-permute-done.16
  193.4 3.7 fusion.16
  197.1 3.7 fusion.15
  200.8 1.3 collective-permute-start.18
  202.2 2.6 collective-permute-done.18
  204.8 1.1 collective-permute-start.19
  205.9 5.9 %add_convert_fusion.1 = bf16[1024,1536]{1,0:T(8,128)(2,1)} fusion(bf16[1024,384]{1,0:T(8,128)(2,1)S(1)} %copy-done.40, bf16[384,1536]{1,0:T(8,128)(2,1)S(1)} %copy-done.35, bf16[2048,1536]{1,0:T(8,128)(2,1)} %collective-permute-done.17), kind=kOutput, calls=%fused_computation.5 | convolution fusion | flops 1212678144 | bytes 8257536 | tf_op jit(solution)/shard_map/dot_general | solution.py:217
  212.6 6.3 %fusion.17 = bf16[384,1536]{1,0:T(8,128)(2,1)} fusion(bf16[4096,1536]{1,0:T(8,128)(2,1)S(1)} %bitcast.85, bf16[4096,384]{1,0:T(8,128)(2,1)S(1)} %copy-done.39, f32[4096]{0:T(1024)S(1)} %bitcast.80), kind=kOutput, calls=%fused_computation.34 | convolution fusion | flops 4837146624 | bytes 16924672 | tf_op jit(solution)/shard_map/te,td->ed/dot_general | solution.py:941
  219.0 1.6 collective-permute-start.20
  221.2 57.4 %backward_blocks.1 = (bf16[4096,1152]{1,0:T(8,128)(2,1)}, bf16[2048,1152]{1,0:T(8,128)(2,1)}, bf16[512,1152]{1,0:T(8,128)(2,1)}, bf16[512,1152]{1,0:T(8,128)(2,1...) custom-call(s32[1]{0:T(128)} %bitcast.place_ref, ...), custom_call_target="tpu_custom_call" | custom-call | flops 61599997952 | bytes 62914560 | tf_op jit(solution)/shard_map/backward_blocks/pallas_call | solution.py:749
  278.7 3.5 add_convert_fusion.4
  282.2 12.8 %convolution_convert_fusion.1 = bf16[2048,1536]{1,0:T(8,128)(2,1)} fusion(bf16[2048,1152]{1,0:T(8,128)(2,1)} %get-tuple-element.216, bf16[1536,1152]{1,0:T(8,128)(2,1)S(1)} %copy-done.5), kind=kOutput, calls=%fused_computation.1 | convolution fusion | flops 7250903040 | bytes 14548992 | tf_op jit(solution)/shard_map/tf,df->td/dot_general | solution.py:954
  295.0 1.4 collective-permute-start.22
  296.8 20.6 %convolution_convert_fusion = bf16[1536,1152]{1,0:T(8,128)(2,1)} fusion(bf16[4096,1536]{1,0:T(8,128)(2,1)} %get-tuple-element.193, bf16[4096,1152]{1,0:T(8,128)(2,1)S(1)} %copy-done.42), kind=kOutput, calls=%fused_computation | convolution fusion | flops 14497284096 | bytes 25559040 | tf_op jit(solution)/shard_map/td,tf->df/dot_general | solution.py:957
  317.8 5.2 %fusion.14 = bf16[512,1536]{1,0:T(8,128)(2,1)} fusion(bf16[512,1152]{1,0:T(8,128)(2,1)} %get-tuple-element.234, bf16[1536,1152]{1,0:T(8,128)(2,1)S(1)} %copy-done.5, bf16[2048,1536]{1,0:T(8,128)(2,1)} %collective-permute-done.24), kind=kOutput, calls=%fused_computation.31 | convolution fusion | flops 1814298624 | bytes 7864320 | tf_op jit(solution)/shard_map/tf,df->td/dot_general | solution.py:954
  323.0 5.3 %fusion.13 = bf16[512,1536]{1,0:T(8,128)(2,1)} fusion(bf16[512,1152]{1,0:T(8,128)(2,1)S(1)} %copy-done.41, bf16[1536,1152]{1,0:T(8,128)(2,1)S(1)} %copy-done.5, bf16[2048,1536]{1,0:T(8,128)(2,1)} %collective-permute-done.24), kind=kOutput, calls=%fused_computation.30 | convolution fusion | flops 1814298624 | bytes 7864320 | tf_op jit(solution)/shard_map/tf,df->td/dot_general | solution.py:954
  328.4 6.1 %add_convert_fusion = bf16[1024,1536]{1,0:T(8,128)(2,1)S(1)} fusion(bf16[1024,1152]{1,0:T(8,128)(2,1)S(1)} %copy-done.43, bf16[1536,1152]{1,0:T(8,128)(2,1)S(1)} %copy-done.6, bf16[2048,1536]{1,0:T(8,128)(2,1)} %collective-permute-done.24), kind=kOutput, calls=%fused_computation.4 | convolution fusion | flops 3628597248 | bytes 12189696 | tf_op jit(solution)/shard_map/tf,df->td/dot_general | solution.py:954
  334.5 1.4 collective-permute-start.25
  336.4 1.0 multiply_reduce_fusion
  339.2 1.8 collective-permute-start.28
  341.1 40.1 %collective-permute-done.25 = bf16[512,1536]{1,0:T(8,128)(2,1)} collective-permute-done((bf16[512,1536]{1,0:T(8,128)(2,1)}, bf16[512,1536]{1,0:T(8,128)(2,1)}, u32[]{:S(2)}, u32[]{:S(2)}) %collective-permute-start.25) | collective-permute-done | bytes 1572896 | tf_op jit(solution)/shard_map/ppermute | solution.py:24
  381.2 2.9 add_convert_fusion.2
  384.1 4.3 collective-permute-start.30
  388.5 2.0 collective-permute-start.31
  390.5 23.7 %collective-permute-done.31 = f32[168,128]{1,0:T(8,128)S(1)} collective-permute-done((f32[168,128]{1,0:T(8,128)S(1)}, f32[168,128]{1,0:T(8,128)S(1)}, u32[]{:S(2)}, u32[]{:S(2)}) %collective-permute-start.31) | collective-permute-done | bytes 86048 | tf_op jit(solution)/shard_map/ppermute | solution.py:24
  414.4 3.1 add_bitcast_fusion.1
  417.5 1.8 collective-permute-start.33
  419.6 1.9 convert_add_fusion.2
  423.6 3.9 collective-permute-done.34
  427.5 7.8 %collective-permute-start.35 = (f32[168,128]{1,0:T(8,128)S(1)}, f32[168,128]{1,0:T(8,128)S(1)}, u32[]{:S(2)}, u32[]{:S(2)}) collective-permute-start(f32[168,128]{1,0:T(8,128)S(1)} %add.209), channel_id=1, source_target_pairs={{0,16},{8,24},{16,0},{24,8},{1,17},{9,25},{17,1},{25,9},{2,18},{10... | collective-permute-start | bytes 258056 | tf_op jit(solution)/shard_map/ppermute | solution.py:24
  435.3 4.7 collective-permute-done.36
  440.3 3.4 fusion.8
  445.0 1.5 reshape.221
  446.5 1.4 fusion.29
  447.9 1.3 slice_bitcast_fusion.3
  449.2 1.3 slice_bitcast_fusion.2
  450.5 1.6 pad_maximum_fusion.piece_ref
  452.1 6.2 %assemble_out_weight_grad.1 = f32[768,1536]{1,0:T(8,128)} custom-call(s32[1]{0:T(128)} %bitcast.place_ref, bf16[8,96,1536]{2,1,0:T(8,128)(2,1)} %pad_maximum_fusion.piece_ref), custom_call_target="tpu_custom_call" | custom-call | flops 5500000256 | bytes 7077888 | tf_op jit(solution)/shard_map/assemble_out_weight_grad/pallas_call | solution.py:805
  458.3 17.6 %all-gather.6.cloned.1.call-done = bf16[3072,1152]{1,0:T(8,128)(2,1)} async-done(((bf16[384,1152]{1,0:T(8,128)(2,1)}), bf16[3072,1152]{1,0:T(8,128)(2,1)}) %all-gather.6.cloned.1.call-update) | async-done | bytes 7077904 | tf_op jit(solution)/shard_map/all_gather | solution.py:1007
  476.0 8.2 %assemble_in_weight_grad.1 = f32[6448,384]{1,0:T(8,128)} custom-call(bf16[8,384,1152]{2,1,0:T(8,128)(2,1)} %bitcast.82), custom_call_target="tpu_custom_call" | custom-call | flops 8800000000 | bytes 14856192 | tf_op jit(solution)/shard_map/assemble_in_weight_grad/pallas_call | solution.py:839
  (235 shorter events, 21.6 us)
Async XLA Ops:
  7.2 88.1 %all-gather.4.cloned.1.call-start = ((), (), s32[]{:S(2)}) async-start(), calls=%async_computation.2 | async-start | bytes 4423680 | tf_op jit(solution)/shard_map/all_gather | solution.py:895
  11.8 149.2 %all-reduce.6.cloned.1.call-start = ((), (), s32[]{:S(2)}) async-start(), calls=%async_computation.3 | async-start | bytes 2359296 | tf_op jit(solution)/shard_map/psum | solution.py:192
  14.3 20.5 %collective-permute-start = (bf16[256,1536]{1,0:T(8,128)(2,1)S(1)}, bf16[256,1536]{1,0:T(8,128)(2,1)S(1)}, u32[]{:S(2)}, u32[]{:S(2)}) collective-permute-start(bf16[256,1536]{1,0:T(8,128)(2,1)S(1)} %get-tuple-element.286), channel_id=1, source_target_pairs={{0,2},{1,3},{2,0},{3,1},{4,6},{5,7},{6,4},{7,5},{8,10},{9,11},{10,... | collective-permute-start | bytes 2359304 | tf_op jit(solution)/shard_map/ppermute | solution.py:24
  17.3 19.6 %collective-permute-start.3 = (bf16[256,1536]{1,0:T(8,128)(2,1)S(1)}, bf16[256,1536]{1,0:T(8,128)(2,1)S(1)}, u32[]{:S(2)}, u32[]{:S(2)}) collective-permute-start(bf16[256,1536]{1,0:T(8,128)(2,1)S(1)} %get-tuple-element.285), channel_id=1, source_target_pairs={{0,4},{1,5},{2,6},{3,7},{4,0},{5,1},{6,2},{7,3},{8,12},{9,13},{10,... | collective-permute-start | bytes 2359304 | tf_op jit(solution)/shard_map/ppermute | solution.py:24
  35.0 3.9 collective-permute-start.2
  35.1 36.9 %collective-permute-start.1 = (bf16[512,1536]{1,0:T(8,128)(2,1)S(1)}, bf16[512,1536]{1,0:T(8,128)(2,1)}, u32[]{:S(2)}, u32[]{:S(2)}) collective-permute-start(bf16[512,1536]{1,0:T(8,128)(2,1)S(1)} %pad_maximum_fusion.1.refs_0_), channel_id=1, source_target_pairs={{0,4},{1,5},{2,6},{3,7},{4,0},{5,1},{6,2},{7,3},{8,12},{9,13},{10,... | collective-permute-start | bytes 4718600 | tf_op jit(solution)/shard_map/ppermute | solution.py:24
  37.0 35.0 %copy-start.10 = (bf16[512,1536]{1,0:T(8,128)(2,1)}, bf16[512,1536]{1,0:T(8,128)(2,1)S(1)}, u32[]{:S(2)}) copy-start(bf16[512,1536]{1,0:T(8,128)(2,1)S(1)} %pad_maximum_fusion.2.refs_4_) | copy-start | bytes 4718596
  37.0 39.9 %copy-start.36 = (f32[48]{0:T(128)S(1)}, f32[48]{0:T(128)}, u32[]{:S(2)}) copy-start(f32[48]{0:T(128)} %param.18) | copy-start | bytes 580
  37.1 40.0 %copy-start.27 = (f32[48]{0:T(128)S(1)}, f32[48]{0:T(128)}, u32[]{:S(2)}) copy-start(f32[48]{0:T(128)} %param.17) | copy-start | bytes 580
  37.1 40.0 %copy-start.28 = (f32[48]{0:T(128)S(1)}, f32[48]{0:T(128)}, u32[]{:S(2)}) copy-start(f32[48]{0:T(128)} %param.16) | copy-start | bytes 580
  37.1 40.9 %copy-start.23 = (f32[3328]{0:T(1024)S(1)}, f32[3328]{0:T(1024)}, u32[]{:S(2)}) copy-start(f32[3328]{0:T(1024)} %param.15) | copy-start | bytes 39940
  37.1 41.0 %slice-start.1 = ((f32[3328]{0:T(1024)}), f32[256]{0:T(256)S(1)}, s32[]{:S(2)}) async-start(f32[3328]{0:T(1024)} %param.15), calls=%async_computation.8 | async-start | bytes 2048 | tf_op jit(solution)/shard_map/slice | solution.py:880
  37.1 41.8 %copy-start.19 = (f32[4,3328]{1,0:T(4,128)S(1)}, f32[4,3328]{1,0:T(4,128)}, u32[]{:S(2)}) copy-start(f32[4,3328]{1,0:T(4,128)} %param.14) | copy-start | bytes 159748
  37.1 41.8 %slice-start = ((f32[4,3328]{1,0:T(4,128)}), f32[4,256]{1,0:T(4,128)S(1)}, s32[]{:S(2)}) async-start(f32[4,3328]{1,0:T(4,128)} %param.14), calls=%async_computation.7 | async-start | bytes 8192 | tf_op jit(solution)/shard_map/slice | solution.py:880
  37.1 34.9 %collective-permute-start.5 = (bf16[512,1536]{1,0:T(8,128)(2,1)S(1)}, bf16[512,1536]{1,0:T(8,128)(2,1)S(1)}, u32[]{:S(2)}, u32[]{:S(2)}) collective-permute-start(bf16[512,1536]{1,0:T(8,128)(2,1)S(1)} %pad_maximum_fusion.2.refs_4_), channel_id=1, source_target_pairs={{0,1},{1,0},{2,3},{3,2},{4,5},{5,4},{6,7},{7,6},{8,9},{9,8},{10,11... | collective-permute-start | bytes 4718600 | tf_op jit(solution)/shard_map/ppermute | solution.py:24
  37.4 36.7 %collective-permute-start.4 = (bf16[512,1536]{1,0:T(8,128)(2,1)S(1)}, bf16[512,1536]{1,0:T(8,128)(2,1)}, u32[]{:S(2)}, u32[]{:S(2)}) collective-permute-start(bf16[512,1536]{1,0:T(8,128)(2,1)S(1)} %pad_maximum_fusion.2.refs_4_), channel_id=1, source_target_pairs={{0,2},{1,3},{2,0},{3,1},{4,6},{5,7},{6,4},{7,5},{8,10},{9,11},{10,... | collective-permute-start | bytes 4718600 | tf_op jit(solution)/shard_map/ppermute | solution.py:24
  39.0 35.7 %copy-start.29 = (bf16[512,1536]{1,0:T(8,128)(2,1)}, bf16[512,1536]{1,0:T(8,128)(2,1)S(1)}, u32[]{:S(2)}) copy-start(bf16[512,1536]{1,0:T(8,128)(2,1)S(1)} %collective-permute-done.2.refs_2_) | copy-start | bytes 4718596
  74.1 21.2 %collective-permute-start.6 = (bf16[512,1536]{1,0:T(8,128)(2,1)}, bf16[512,1536]{1,0:T(8,128)(2,1)}, u32[]{:S(2)}, u32[]{:S(2)}) collective-permute-start(bf16[512,1536]{1,0:T(8,128)(2,1)} %collective-permute-done.1.refs_1_), channel_id=1, source_target_pairs={{0,1},{1,0},{2,3},{3,2},{4,5},{5,4},{6,7},{7,6},{8,9},{9,8},{10,11... | collective-permute-start | bytes 4718600 | tf_op jit(solution)/shard_map/ppermute | solution.py:24
  74.1 21.2 %collective-permute-start.7 = (bf16[512,1536]{1,0:T(8,128)(2,1)}, bf16[512,1536]{1,0:T(8,128)(2,1)}, u32[]{:S(2)}, u32[]{:S(2)}) collective-permute-start(bf16[512,1536]{1,0:T(8,128)(2,1)} %collective-permute-done.4.refs_5_), channel_id=1, source_target_pairs={{0,1},{1,0},{2,3},{3,2},{4,5},{5,4},{6,7},{7,6},{8,9},{9,8},{10,11... | collective-permute-start | bytes 4718600 | tf_op jit(solution)/shard_map/ppermute | solution.py:24
  74.6 19.4 %collective-permute-start.8 = (bf16[256,1536]{1,0:T(8,128)(2,1)S(1)}, bf16[256,1536]{1,0:T(8,128)(2,1)S(1)}, u32[]{:S(2)}, u32[]{:S(2)}) collective-permute-start(bf16[256,1536]{1,0:T(8,128)(2,1)S(1)} %get-tuple-element.162), channel_id=1, source_target_pairs={{0,2},{1,3},{2,0},{3,1},{4,6},{5,7},{6,4},{7,5},{8,10},{9,11},{10,... | collective-permute-start | bytes 2359304 | tf_op jit(solution)/shard_map/ppermute | solution.py:24
  76.1 19.2 %collective-permute-start.9 = (bf16[256,1536]{1,0:T(8,128)(2,1)S(1)}, bf16[256,1536]{1,0:T(8,128)(2,1)S(1)}, u32[]{:S(2)}, u32[]{:S(2)}) collective-permute-start(bf16[256,1536]{1,0:T(8,128)(2,1)S(1)} %get-tuple-element.164), channel_id=1, source_target_pairs={{0,4},{1,5},{2,6},{3,7},{4,0},{5,1},{6,2},{7,3},{8,12},{9,13},{10,... | collective-permute-start | bytes 2359304 | tf_op jit(solution)/shard_map/ppermute | solution.py:24
  97.3 63.8 %collective-permute-start.13 = (bf16[512,1536]{1,0:T(8,128)(2,1)}, bf16[512,1536]{1,0:T(8,128)(2,1)}, u32[]{:S(2)}, u32[]{:S(2)}) collective-permute-start(bf16[512,1536]{1,0:T(8,128)(2,1)} %constant_dynamic-update-slice_fusion.2.refs_4_), channel_id=1, source_target_pairs={{0,1},{1,0},{2,3},{3,2},{4,5},{5,4},{6,7},{7,6},{8,9},{9,8},{10,11... | collective-permute-start | bytes 4718600 | tf_op jit(solution)/shard_map/ppermute | solution.py:24
  97.3 63.8 %collective-permute-start.12 = (bf16[512,1536]{1,0:T(8,128)(2,1)}, bf16[512,1536]{1,0:T(8,128)(2,1)}, u32[]{:S(2)}, u32[]{:S(2)}) collective-permute-start(bf16[512,1536]{1,0:T(8,128)(2,1)} %constant_dynamic-update-slice_fusion.2.refs_4_), channel_id=1, source_target_pairs={{0,2},{1,3},{2,0},{3,1},{4,6},{5,7},{6,4},{7,5},{8,10},{9,11},{10,... | collective-permute-start | bytes 4718600 | tf_op jit(solution)/shard_map/ppermute | solution.py:24
  99.7 61.4 %collective-permute-start.11 = (bf16[512,1536]{1,0:T(8,128)(2,1)}, bf16[512,1536]{1,0:T(8,128)(2,1)S(1)}, u32[]{:S(2)}, u32[]{:S(2)}) collective-permute-start(bf16[512,1536]{1,0:T(8,128)(2,1)} %constant_dynamic-update-slice_fusion.refs_0_), channel_id=1, source_target_pairs={{0,1},{1,0},{2,3},{3,2},{4,5},{5,4},{6,7},{7,6},{8,9},{9,8},{10,11... | collective-permute-start | bytes 4718600 | tf_op jit(solution)/shard_map/ppermute | solution.py:24
  99.9 61.2 %collective-permute-start.10 = (bf16[512,1536]{1,0:T(8,128)(2,1)}, bf16[512,1536]{1,0:T(8,128)(2,1)S(1)}, u32[]{:S(2)}, u32[]{:S(2)}) collective-permute-start(bf16[512,1536]{1,0:T(8,128)(2,1)} %constant_dynamic-update-slice_fusion.refs_0_), channel_id=1, source_target_pairs={{0,4},{1,5},{2,6},{3,7},{4,0},{5,1},{6,2},{7,3},{8,12},{9,13},{10,... | collective-permute-start | bytes 4718600 | tf_op jit(solution)/shard_map/ppermute | solution.py:24
  102.2 180.0 %reduce-scatter.3.cloned.1.call-start = ((), (), s32[]{:S(2)}) async-start(), calls=%async_computation.4 | async-start | bytes 1474560 | tf_op jit(solution)/shard_map/reduce_scatter | solution.py:943
  161.1 9.0 %copy-start.31 = (bf16[512,1536]{1,0:T(8,128)(2,1)}, bf16[512,1536]{1,0:T(8,128)(2,1)S(1)}, u32[]{:S(2)}) copy-start(bf16[512,1536]{1,0:T(8,128)(2,1)S(1)} %collective-permute-done.11.refs_2_) | copy-start | bytes 4718596
  161.1 9.0 %copy-start.32 = (bf16[512,1536]{1,0:T(8,128)(2,1)}, bf16[512,1536]{1,0:T(8,128)(2,1)S(1)}, u32[]{:S(2)}) copy-start(bf16[512,1536]{1,0:T(8,128)(2,1)S(1)} %collective-permute-done.10.refs_1_) | copy-start | bytes 4718596
  161.1 9.0 %collective-permute-start.14 = (bf16[512,1536]{1,0:T(8,128)(2,1)S(1)}, bf16[512,1536]{1,0:T(8,128)(2,1)S(1)}, u32[]{:S(2)}, u32[]{:S(2)}) collective-permute-start(bf16[512,1536]{1,0:T(8,128)(2,1)S(1)} %collective-permute-done.10.refs_1_), channel_id=1, source_target_pairs={{0,1},{1,0},{2,3},{3,2},{4,5},{5,4},{6,7},{7,6},{8,9},{9,8},{10,11... | collective-permute-start | bytes 4718600 | tf_op jit(solution)/shard_map/ppermute | solution.py:24
  161.2 8.9 %collective-permute-start.15 = (bf16[512,1536]{1,0:T(8,128)(2,1)}, bf16[512,1536]{1,0:T(8,128)(2,1)S(1)}, u32[]{:S(2)}, u32[]{:S(2)}) collective-permute-start(bf16[512,1536]{1,0:T(8,128)(2,1)} %collective-permute-done.12.refs_5_), channel_id=1, source_target_pairs={{0,1},{1,0},{2,3},{3,2},{4,5},{5,4},{6,7},{7,6},{8,9},{9,8},{10,11... | collective-permute-start | bytes 4718600 | tf_op jit(solution)/shard_map/ppermute | solution.py:24
  170.1 23.2 %collective-permute-start.17 = (bf16[2048,1536]{1,0:T(8,128)(2,1)}, bf16[2048,1536]{1,0:T(8,128)(2,1)}, u32[]{:S(2)}, u32[]{:S(2)}) collective-permute-start(bf16[2048,1536]{1,0:T(8,128)(2,1)} %convolution_convert_fusion.2), channel_id=1, source_target_pairs={{0,1},{1,0},{2,3},{3,2},{4,5},{5,4},{6,7},{7,6},{8,9},{9,8},{10,11... | collective-permute-start | bytes 18874376 | tf_op jit(solution)/shard_map/ppermute | solution.py:24
  172.7 20.7 %copy-start.35 = (bf16[384,1536]{1,0:T(8,128)(2,1)S(1)}, bf16[384,1536]{1,0:T(8,128)(2,1)}, u32[]{:S(2)}) copy-start(bf16[384,1536]{1,0:T(8,128)(2,1)} %all-reduce.6.cloned.1.call-done.refs_9_) | copy-start | bytes 3538948
  172.7 20.7 %copy-start.38 = (bf16[512,384]{1,0:T(8,128)(2,1)S(1)}, bf16[512,384]{1,0:T(8,128)(2,1)}, u32[]{:S(2)}) copy-start(bf16[512,384]{1,0:T(8,128)(2,1)} %get-tuple-element.187) | copy-start | bytes 1179652
  192.0 1.3 collective-permute-start.16
  193.4 19.2 %slice-start.2 = ((s8[12582912]{0:T(1024)(128)(4,1)}), s8[4194304]{0:T(1024)(128)(4,1)S(1)}, s32[]{:S(2)}) async-start(s8[12582912]{0:T(1024)(128)(4,1)} %bitcast.84), calls=%async_computation.9 | async-start | bytes 8388608
  197.1 8.8 %copy-start.40 = (bf16[1024,384]{1,0:T(8,128)(2,1)S(1)}, bf16[1024,384]{1,0:T(8,128)(2,1)}, u32[]{:S(2)}) copy-start(bf16[1024,384]{1,0:T(8,128)(2,1)} %get-tuple-element.212) | copy-start | bytes 2359300
  197.1 15.5 %slice-start.3 = ((s8[12582912]{0:T(1024)(128)(4,1)}), s8[4194304]{0:T(1024)(128)(4,1)S(1)}, s32[]{:S(2)}) async-start(s8[12582912]{0:T(1024)(128)(4,1)} %bitcast.84), calls=%async_computation.10 | async-start | bytes 8388608
  200.8 3.9 collective-permute-start.18
  204.8 7.0 %collective-permute-start.19 = (f32[2,4096]{1,0:T(2,128)S(1)}, f32[2,4096]{1,0:T(2,128)S(1)}, u32[]{:S(2)}, u32[]{:S(2)}) collective-permute-start(f32[2,4096]{1,0:T(2,128)S(1)} %add.183), channel_id=1, source_target_pairs={{0,4},{1,5},{2,6},{3,7},{4,0},{5,1},{6,2},{7,3},{8,12},{9,13},{10,... | collective-permute-start | bytes 98312 | tf_op jit(solution)/shard_map/ppermute | solution.py:24
  218.9 195.4 %reduce-scatter.5.cloned.1.call-start = ((), (), s32[]{:S(2)}) async-start(), calls=%async_computation.5 | async-start | bytes 4423680 | tf_op jit(solution)/shard_map/reduce_scatter | solution.py:965
  219.0 59.7 %collective-permute-start.20 = (bf16[512,1536]{1,0:T(8,128)(2,1)}, bf16[512,1536]{1,0:T(8,128)(2,1)}, u32[]{:S(2)}, u32[]{:S(2)}) collective-permute-start(bf16[512,1536]{1,0:T(8,128)(2,1)} %fusion.15), channel_id=1, source_target_pairs={{0,2},{1,3},{2,0},{3,1},{4,6},{5,7},{6,4},{7,5},{8,10},{9,11},{10,... | collective-permute-start | bytes 4718600 | tf_op jit(solution)/shard_map/ppermute | solution.py:24
  220.5 58.1 %collective-permute-start.21 = (bf16[512,1536]{1,0:T(8,128)(2,1)}, bf16[512,1536]{1,0:T(8,128)(2,1)}, u32[]{:S(2)}, u32[]{:S(2)}) collective-permute-start(bf16[512,1536]{1,0:T(8,128)(2,1)} %fusion.16), channel_id=1, source_target_pairs={{0,4},{1,5},{2,6},{3,7},{4,0},{5,1},{6,2},{7,3},{8,12},{9,13},{10,... | collective-permute-start | bytes 4718600 | tf_op jit(solution)/shard_map/ppermute | solution.py:24
  282.2 14.6 %copy-start.42 = (bf16[4096,1152]{1,0:T(8,128)(2,1)S(1)}, bf16[4096,1152]{1,0:T(8,128)(2,1)}, u32[]{:S(2)}) copy-start(bf16[4096,1152]{1,0:T(8,128)(2,1)} %get-tuple-element.218) | copy-start | bytes 28311556
  295.0 22.8 %collective-permute-start.24 = (bf16[2048,1536]{1,0:T(8,128)(2,1)}, bf16[2048,1536]{1,0:T(8,128)(2,1)}, u32[]{:S(2)}, u32[]{:S(2)}) collective-permute-start(bf16[2048,1536]{1,0:T(8,128)(2,1)} %convolution_convert_fusion.1), channel_id=1, source_target_pairs={{0,1},{1,0},{2,3},{3,2},{4,5},{5,4},{6,7},{7,6},{8,9},{9,8},{10,11... | collective-permute-start | bytes 18874376 | tf_op jit(solution)/shard_map/ppermute | solution.py:24
  295.0 22.5 %collective-permute-start.22 = (bf16[256,1536]{1,0:T(8,128)(2,1)}, bf16[256,1536]{1,0:T(8,128)(2,1)}, u32[]{:S(2)}, u32[]{:S(2)}) collective-permute-start(bf16[256,1536]{1,0:T(8,128)(2,1)} %get-tuple-element.223), channel_id=1, source_target_pairs={{0,4},{1,5},{2,6},{3,7},{4,0},{5,1},{6,2},{7,3},{8,12},{9,13},{10,... | collective-permute-start | bytes 2359304 | tf_op jit(solution)/shard_map/ppermute | solution.py:24
  296.3 21.1 %collective-permute-start.23 = (bf16[256,1536]{1,0:T(8,128)(2,1)}, bf16[256,1536]{1,0:T(8,128)(2,1)}, u32[]{:S(2)}, u32[]{:S(2)}) collective-permute-start(bf16[256,1536]{1,0:T(8,128)(2,1)} %get-tuple-element.225), channel_id=1, source_target_pairs={{0,2},{1,3},{2,0},{3,1},{4,6},{5,7},{6,4},{7,5},{8,10},{9,11},{10,... | collective-permute-start | bytes 2359304 | tf_op jit(solution)/shard_map/ppermute | solution.py:24
  317.5 158.5 %all-gather.6.cloned.1.call-start = ((), (), s32[]{:S(2)}) async-start(), calls=%async_computation.6 | async-start | bytes 7962624 | tf_op jit(solution)/shard_map/all_gather | solution.py:1007
  328.4 8.0 %copy-start.2 = (bf16[1536,1152]{1,0:T(8,128)(2,1)S(1)}, bf16[1536,1152]{1,0:T(8,128)(2,1)}, u32[]{:S(2)}) copy-start(bf16[1536,1152]{1,0:T(8,128)(2,1)} %convolution_convert_fusion) | copy-start | bytes 10616836
  334.4 46.8 %copy-start.7 = (bf16[1024,1536]{1,0:T(8,128)(2,1)}, bf16[1024,1536]{1,0:T(8,128)(2,1)S(1)}, u32[]{:S(2)}) copy-start(bf16[1024,1536]{1,0:T(8,128)(2,1)S(1)} %add_convert_fusion) | copy-start | bytes 9437188
  334.5 46.7 %collective-permute-start.25 = (bf16[512,1536]{1,0:T(8,128)(2,1)}, bf16[512,1536]{1,0:T(8,128)(2,1)}, u32[]{:S(2)}, u32[]{:S(2)}) collective-permute-start(bf16[512,1536]{1,0:T(8,128)(2,1)} %fusion.13), channel_id=1, source_target_pairs={{0,2},{1,3},{2,0},{3,1},{4,6},{5,7},{6,4},{7,5},{8,10},{9,11},{10,... | collective-permute-start | bytes 4718600 | tf_op jit(solution)/shard_map/ppermute | solution.py:24
  335.9 45.3 %collective-permute-start.26 = (bf16[512,1536]{1,0:T(8,128)(2,1)}, bf16[512,1536]{1,0:T(8,128)(2,1)}, u32[]{:S(2)}, u32[]{:S(2)}) collective-permute-start(bf16[512,1536]{1,0:T(8,128)(2,1)} %fusion.14), channel_id=1, source_target_pairs={{0,4},{1,5},{2,6},{3,7},{4,0},{5,1},{6,2},{7,3},{8,12},{9,13},{10,... | collective-permute-start | bytes 4718600 | tf_op jit(solution)/shard_map/ppermute | solution.py:24
  339.1 1.9 collective-permute-start.27
  339.2 44.9 %collective-permute-start.28 = (bf16[96,1536]{1,0:T(8,128)(2,1)}, bf16[96,1536]{1,0:T(8,128)(2,1)S(1)}, u32[]{:S(2)}, u32[]{:S(2)}) collective-permute-start(bf16[96,1536]{1,0:T(8,128)(2,1)} %reduce-scatter.3.cloned.1.call-done), channel_id=1, source_target_pairs={{0,0},{1,1},{8,2},{9,3},{16,4},{17,5},{24,6},{25,7},{2,8},{3,9},{1... | collective-permute-start | bytes 884744 | tf_op jit(solution)/shard_map/ppermute | solution.py:196
  384.1 30.2 %collective-permute-start.29 = (bf16[256,1536]{1,0:T(8,128)(2,1)}, bf16[256,1536]{1,0:T(8,128)(2,1)S(1)}, u32[]{:S(2)}, u32[]{:S(2)}) collective-permute-start(bf16[256,1536]{1,0:T(8,128)(2,1)} %get-tuple-element.258), channel_id=1, source_target_pairs={{0,4},{1,5},{2,6},{3,7},{4,0},{5,1},{6,2},{7,3},{8,12},{9,13},{10,... | collective-permute-start | bytes 2359304 | tf_op jit(solution)/shard_map/ppermute | solution.py:24
  384.1 30.2 %collective-permute-start.30 = (bf16[256,1536]{1,0:T(8,128)(2,1)}, bf16[256,1536]{1,0:T(8,128)(2,1)S(1)}, u32[]{:S(2)}, u32[]{:S(2)}) collective-permute-start(bf16[256,1536]{1,0:T(8,128)(2,1)} %get-tuple-element.259), channel_id=1, source_target_pairs={{0,2},{1,3},{2,0},{3,1},{4,6},{5,7},{6,4},{7,5},{8,10},{9,11},{10,... | collective-permute-start | bytes 2359304 | tf_op jit(solution)/shard_map/ppermute | solution.py:24
  388.5 25.8 %collective-permute-start.32 = (bf16[1,96,1536]{2,1,0:T(8,128)(2,1)S(1)}, bf16[1,96,1536]{2,1,0:T(8,128)(2,1)S(1)}, u32[]{:S(2)}, u32[]{:S(2)}) collective-permute-start(bf16[1,96,1536]{2,1,0:T(8,128)(2,1)S(1)} %bitcast.73), channel_id=1, source_target_pairs={{0,2},{1,3},{2,0},{3,1},{4,6},{5,7},{6,4},{7,5},{8,10},{9,11},{10,... | collective-permute-start | bytes 884744 | tf_op jit(solution)/shard_map/ppermute | solution.py:24
  388.5 25.7 %collective-permute-start.31 = (f32[168,128]{1,0:T(8,128)S(1)}, f32[168,128]{1,0:T(8,128)S(1)}, u32[]{:S(2)}, u32[]{:S(2)}) collective-permute-start(f32[168,128]{1,0:T(8,128)S(1)} %fusion.25), channel_id=1, source_target_pairs={{0,2},{1,3},{2,0},{3,1},{4,6},{5,7},{6,4},{7,5},{8,10},{9,11},{10,... | collective-permute-start | bytes 258056 | tf_op jit(solution)/shard_map/ppermute | solution.py:24
  417.5 5.4 %collective-permute-start.33 = (f32[168,128]{1,0:T(8,128)S(1)}, f32[168,128]{1,0:T(8,128)S(1)}, u32[]{:S(2)}, u32[]{:S(2)}) collective-permute-start(f32[168,128]{1,0:T(8,128)S(1)} %add.202), channel_id=1, source_target_pairs={{0,4},{1,5},{2,6},{3,7},{4,0},{5,1},{6,2},{7,3},{8,12},{9,13},{10,... | collective-permute-start | bytes 258056 | tf_op jit(solution)/shard_map/ppermute | solution.py:24
  419.3 20.8 %collective-permute-start.36 = (bf16[2,96,1536]{2,1,0:T(8,128)(2,1)S(1)}, bf16[2,96,1536]{2,1,0:T(8,128)(2,1)S(1)}, u32[]{:S(2)}, u32[]{:S(2)}) collective-permute-start(bf16[2,96,1536]{2,1,0:T(8,128)(2,1)S(1)} %pad_maximum_fusion.4), channel_id=1, source_target_pairs={{0,4},{1,5},{2,6},{3,7},{4,0},{5,1},{6,2},{7,3},{8,12},{9,13},{10,... | collective-permute-start | bytes 1769480 | tf_op jit(solution)/shard_map/ppermute | solution.py:24
  422.0 18.2 %copy-start.4 = (bf16[1,512,1536]{2,1,0:T(8,128)(2,1)S(1)}, bf16[1,512,1536]{2,1,0:T(8,128)(2,1)}, u32[]{:S(2)}) copy-start(bf16[1,512,1536]{2,1,0:T(8,128)(2,1)} %param.21) | copy-start | bytes 4718596
  422.0 18.2 %copy-start.18 = (f32[512]{0:T(512)S(1)}, f32[512]{0:T(512)}, u32[]{:S(2)}) copy-start(f32[512]{0:T(512)} %copy-done.17) | copy-start | bytes 6148
  422.9 4.6 collective-permute-start.34
  427.5 16.2 %collective-permute-start.35 = (f32[168,128]{1,0:T(8,128)S(1)}, f32[168,128]{1,0:T(8,128)S(1)}, u32[]{:S(2)}, u32[]{:S(2)}) collective-permute-start(f32[168,128]{1,0:T(8,128)S(1)} %add.209), channel_id=1, source_target_pairs={{0,16},{8,24},{16,0},{24,8},{1,17},{9,25},{17,1},{25,9},{2,18},{10... | collective-permute-start | bytes 258056 | tf_op jit(solution)/shard_map/ppermute | solution.py:24
  440.2 10.3 %collective-permute-start.37 = (bf16[4,96,1536]{2,1,0:T(8,128)(2,1)S(1)}, bf16[4,96,1536]{2,1,0:T(8,128)(2,1)S(1)}, u32[]{:S(2)}, u32[]{:S(2)}) collective-permute-start(bf16[4,96,1536]{2,1,0:T(8,128)(2,1)S(1)} %pad_maximum_fusion.3), channel_id=1, source_target_pairs={{0,1},{1,0},{2,3},{3,2},{4,5},{5,4},{6,7},{7,6},{8,9},{9,8},{10,11... | collective-permute-start | bytes 3538952 | tf_op jit(solution)/shard_map/ppermute | solution.py:24
  (28 other events, 94.3 us)
Sparse Core Ops, SparseCore 0:
  12.0 72.6 all-gather.3
  102.3 56.7 all-reduce.5
  219.0 29.6 reduce-scatter.2
  317.6 85.5 reduce-scatter.4
  414.5 61.4 all-gather.5
where the time goes:
time: 500 us; the launch traced here: 491 us
  waiting for transfers between devices  161 us (32%)
  Pallas kernels  148 us (30%)
  matrix products  78 us (16%)
  starting transfers between devices  41.1 us (8%)
  other arithmetic  24.1 us (5%)
  local copies, waits for them, and re-layouts  23.2 us (5%)
  between operations  15 us (3%)
    ppermute x37, waiting for transfers between devices, exchange(): lax.ppermute(value, axis, [(source, source ^ distance) for source in rang...  144 us
    pallas_call x1, Pallas kernels, run_forward(): pl.pallas_call(functools.partial(forward_kernel, dims, table, len(arrays)...  58.1 us
    pallas_call x1, Pallas kernels, run_backward(): pl.pallas_call(functools.partial(backward_kernel, dims), grid_spec=pltpu....  57.4 us
    ppermute x37, starting transfers between devices, exchange(): lax.ppermute(value, axis, [(source, source ^ distance) for source in rang...  38.8 us
    dot_general x4, matrix products, back_product(): return jnp.einsum('tf,df->td', part, w_cols, preferred_element_type=f32)  29.4 us
    dot_general x4, matrix products, dot(): return jnp.dot(a, b, preferred_element_type=f32)  21.6 us
    dot_general x1, matrix products, weight_product(): jnp.einsum('td,tf->df', normed, part, preferred_element_type=f32)  20.6 us
    pallas_call x1, Pallas kernels, run_out_grad(): pl.pallas_call(functools.partial(out_grad_kernel, table, len(arrays)), gr...  18.4 us
  transfers between devices with their start and end apart: 43, of which 13 were waited for; matrix products, arithmetic and copies ran while one was open for 18% of the time, Pallas kernels for 29%

commit v1 on v0

--- a/solution.py
+++ b/solution.py
@@ -242,6 +242,11 @@
         parts.append(part)
         value = value - part.astype(f32)
     return parts
+
+
+def dot_split(product, a, b):
+    first, second = split_parts(b, 2)
+    return product(a, first) + product(a, second)
 
 
 def sum_along(rows, order):
@@ -410,12 +415,11 @@
             jnp.concatenate([dot(near.astype(bf16), part[first]), dot(both, part)], axis=0)
         )
     start = state[...]
-    start_low = start.astype(bf16)
-    start_ref[0] = start_low
-    carried = dot(readout, start_low) * early_wide
+    start_ref[0] = start
+    carried = dot_split(dot, readout, start) * early_wide
     ssd = jnp.concatenate(within, axis=1) + carried + rows_ref[0:1] * signal_wide
-    tail = (signal_wide * tail_wide).astype(bf16)
-    state[...] = start * early_wide[GROUP - 1 :] + dot_tn(entry, tail)
+    tail = signal_wide * tail_wide
+    state[...] = start * early_wide[GROUP - 1 :] + dot_split(dot_tn, entry, tail)
 
     gate_act, gate_slope = silu_slope(projected[:, :width])
     gate_act_ref[...] = gate_act.astype(bf16)
@@ -502,7 +506,7 @@
             jax.ShapeDtypeStruct((tokens, width), bf16),
             jax.ShapeDtypeStruct((blocks, 8, GROUP), f32),
             jax.ShapeDtypeStruct((tokens, width), f32),
-            jax.ShapeDtypeStruct((blocks, states, width), bf16),
+            jax.ShapeDtypeStruct((blocks, states, width), f32),
             jax.ShapeDtypeStruct((tokens, width), bf16),
             jax.ShapeDtypeStruct((blocks, 8, GROUP), f32),
             jax.ShapeDtypeStruct((tokens, dim), bf16),
@@ -639,7 +643,8 @@
     entry = active_ref[:, width : width + states]
     readout = active_ref[:, width + states :]
     signal_wide = signal.astype(f32)
-    start_low = start_ref[0]
+    start = start_ref[0]
+    start_low = start.astype(bf16)
     end_grad = state[...]
     end_low = end_grad.astype(bf16)
     first, second = slice(0, HALF), slice(HALF, GROUP)
@@ -667,26 +672,26 @@
         near_grad = near_grad + cross[:, first] * near
         far_grad = far_grad + cross[:, second] * full
         last_grad = last_grad + dot_nt(part[second], grad[second]) * last
-    tail_grad = tail_wide * dot(entry, end_low)
+    tail_grad = tail_wide * dot_split(dot, entry, end_grad)
     signal_grad = jnp.concatenate(within, axis=1) + tail_grad
     score_first = jnp.concatenate([near_grad, far_grad], axis=1).astype(bf16)
     score_second = last_grad.astype(bf16)
     tail = (signal_wide * tail_wide).astype(bf16)
-    head_grad = (ssd_grad * early_wide).astype(bf16)
+    head_grad = ssd_grad * early_wide
     entry_grad = jnp.concatenate(
         [dot(score_first, readout), dot(score_second, readout[second])], axis=0
     ) + dot_nt(tail, end_low)
-    readout_grad = dot_tn(score_first, entry[first]) + dot_nt(head_grad, start_low)
+    readout_grad = dot_tn(score_first, entry[first]) + dot_nt(head_grad.astype(bf16), start_low)
     readout_last = readout_grad[second] + dot_tn(score_second, entry[second])
     total_wide = early_wide[GROUP - 1 :]
-    state[...] = end_grad * total_wide + dot_tn(readout, head_grad)
+    state[...] = end_grad * total_wide + dot_split(dot_tn, readout, head_grad)
 
     skip = rows_ref[0:1]
     ones = head_ones(width, size)
     column_part = signal_wide * signal_grad
     row_part = ssd_grad * (ssd - skip * signal_wide)
     end_part = jnp.sum(signal_wide * tail_grad, axis=0, keepdims=True) + total_wide * jnp.sum(
-        start_low.astype(f32) * end_grad, axis=0, keepdims=True
+        start * end_grad, axis=0, keepdims=True
     )
 
     def head_sums(value, parts):

time: 500 us -> 500 us (level)
  no operation moved by 1% of the time
where the time goes in v1:
time: 500 us; the launch traced here: 491 us
  waiting for transfers between devices  161 us (32%)
  Pallas kernels  148 us (30%)
  matrix products  78 us (16%)
  starting transfers between devices  41.3 us (8%)
  other arithmetic  24.1 us (5%)
  local copies, waits for them, and re-layouts  23.2 us (5%)
  between operations  15 us (3%)
    ppermute x37, waiting for transfers between devices, exchange(): lax.ppermute(value, axis, [(source, source ^ distance) for source in rang...  143 us
    pallas_call x1, Pallas kernels, run_forward(): pl.pallas_call(functools.partial(forward_kernel, dims, table, len(arrays)...  58.3 us
    pallas_call x1, Pallas kernels, run_backward(): pl.pallas_call(functools.partial(backward_kernel, dims), grid_spec=pltpu....  57.3 us
    ppermute x37, starting transfers between devices, exchange(): lax.ppermute(value, axis, [(source, source ^ distance) for source in rang...  39 us
    dot_general x4, matrix products, back_product(): return jnp.einsum('tf,df->td', part, w_cols, preferred_element_type=f32)  29.4 us
    dot_general x4, matrix products, dot(): return jnp.dot(a, b, preferred_element_type=f32)  21.7 us
    dot_general x1, matrix products, weight_product(): jnp.einsum('td,tf->df', normed, part, preferred_element_type=f32)  20.6 us
    pallas_call x1, Pallas kernels, run_out_grad(): pl.pallas_call(functools.partial(out_grad_kernel, table, len(arrays)), gr...  18.4 us
  transfers between devices with their start and end apart: 43, of which 13 were waited for; matrix products, arithmetic and copies ran while one was open for 18% of the time, Pallas kernels for 29%

profile of v1, /device:TPU:0, one launch (start us, length us, event | category | flops | bytes accessed | tf_op | source)
XLA Modules:
  0.0 491.0 jit_solution(3580554107733893946)
XLA Ops:
  7.2 1.0 slice.151
  9.2 1.1 constant_dynamic-slice_fusion.4
  10.8 1.0 fusion.19
  14.4 3.0 collective-permute-start
  17.4 1.5 collective-permute-start.3
  18.9 16.0 %collective-permute-done = bf16[256,1536]{1,0:T(8,128)(2,1)S(1)} collective-permute-done((bf16[256,1536]{1,0:T(8,128)(2,1)S(1)}, bf16[256,1536]{1,0:T(8,128)(2,1)S(1)}, u32[]{:S(2)}, u32[]{:S(2)}) %collective-permute-start) | collective-permute-done | bytes 786464 | tf_op jit(solution)/shard_map/ppermute | solution.py:24
  35.2 1.8 collective-permute-start.1
  37.4 1.5 collective-permute-start.4
  39.0 33.0 %collective-permute-done.1.refs_1_ = bf16[512,1536]{1,0:T(8,128)(2,1)} collective-permute-done((bf16[512,1536]{1,0:T(8,128)(2,1)S(1)}, bf16[512,1536]{1,0:T(8,128)(2,1)}, u32[]{:S(2)}, u32[]{:S(2)}) %collective-permute-start.1) | collective-permute-done | bytes 1572896 | tf_op jit(solution)/shard_map/ppermute | solution.py:24
  72.1 2.1 collective-permute-done.4.refs_5_
  74.7 1.5 collective-permute-start.8
  80.2 13.9 %collective-permute-done.8 = bf16[256,1536]{1,0:T(8,128)(2,1)S(1)} collective-permute-done((bf16[256,1536]{1,0:T(8,128)(2,1)S(1)}, bf16[256,1536]{1,0:T(8,128)(2,1)S(1)}, u32[]{:S(2)}, u32[]{:S(2)}) %collective-permute-start.8) | collective-permute-done | bytes 786464 | tf_op jit(solution)/shard_map/ppermute | solution.py:24
  94.1 1.2 collective-permute-done.9
  95.4 1.0 constant_dynamic-update-slice_fusion.3
  96.3 0.9 constant_dynamic-update-slice_fusion.2.refs_4_
  97.8 1.0 constant_dynamic-update-slice_fusion.1
  98.8 1.0 constant_dynamic-update-slice_fusion.refs_0_
  100.0 0.9 collective-permute-start.10
  100.9 1.3 dynamic-slice_select_fusion
  103.0 58.3 %forward_blocks.1 = (bf16[4096,640]{1,0:T(8,128)(2,1)}, bf16[4096,640]{1,0:T(8,128)(2,1)}, bf16[4096,640]{1,0:T(8,128)(2,1)}, bf16[4096,384]{1,0:T(8,128)(2,1)},...) custom-call(s32[1]{0:T(128)} %bitcast.place_ref, ...), custom_call_target="tpu_custom_call" | custom-call | flops 52800000000 | bytes 62914560 | tf_op jit(solution)/shard_map/forward_blocks/pallas_call | solution.py:470
  161.9 8.4 %convolution_convert_fusion.2 = bf16[2048,1536]{1,0:T(8,128)(2,1)} fusion(bf16[2048,384]{1,0:T(8,128)(2,1)} %get-tuple-element.167, bf16[384,1536]{1,0:T(8,128)(2,1)} %all-reduce.6.cloned.1.call-done.refs_9_), kind=kOutput, calls=%fused_computation.2 | convolution fusion | flops 2419064832 | bytes 9043968 | tf_op jit(solution)/shard_map/dot_general | solution.py:217
  170.4 1.1 copy-done.33
  172.9 18.4 %out_grad.1 = (f32[4096,384]{1,0:T(8,128)}, f32[16,8,256]{2,1,0:T(8,128)}, bf16[4096,1536]{1,0:T(8,128)(2,1)}) custom-call(s32[1]{0:T(128)} %bitcast.place_ref, bf16[512,1536]{1,0:T(8,128)(2,1)} %constant_dynamic-update-slice_fusion.refs_0_, bf16[512,1536]{1,0:T(8,128)(2,1)} %copy-done.32, bf16[512,1536]{1,0:T(8,128)(2,1)} %copy-done.31, ...), custom_call_target="tpu_custom_call" | custom-call | flops 13200000000 | bytes 34603008 | tf_op jit(solution)/shard_map/out_grad/pallas_call | solution.py:555
  191.2 0.9 slice.161
  192.3 1.2 collective-permute-done.16
  193.6 3.7 fusion.16
  197.2 3.7 fusion.15
  201.0 1.4 collective-permute-start.18
  202.4 2.5 collective-permute-done.18
  204.9 1.1 collective-permute-start.19
  206.1 5.9 %add_convert_fusion.1 = bf16[1024,1536]{1,0:T(8,128)(2,1)} fusion(bf16[1024,384]{1,0:T(8,128)(2,1)S(1)} %copy-done.40, bf16[384,1536]{1,0:T(8,128)(2,1)S(1)} %copy-done.35, bf16[2048,1536]{1,0:T(8,128)(2,1)} %collective-permute-done.17), kind=kOutput, calls=%fused_computation.5 | convolution fusion | flops 1212678144 | bytes 8257536 | tf_op jit(solution)/shard_map/dot_general | solution.py:217
  212.8 6.3 %fusion.17 = bf16[384,1536]{1,0:T(8,128)(2,1)} fusion(bf16[4096,1536]{1,0:T(8,128)(2,1)S(1)} %bitcast.85, bf16[4096,384]{1,0:T(8,128)(2,1)S(1)} %copy-done.39, f32[4096]{0:T(1024)S(1)} %bitcast.80), kind=kOutput, calls=%fused_computation.34 | convolution fusion | flops 4837146624 | bytes 16924672 | tf_op jit(solution)/shard_map/te,td->ed/dot_general | solution.py:946
  219.2 1.6 collective-permute-start.20
  221.5 57.3 %backward_blocks.1 = (bf16[4096,1152]{1,0:T(8,128)(2,1)}, bf16[2048,1152]{1,0:T(8,128)(2,1)}, bf16[512,1152]{1,0:T(8,128)(2,1)}, bf16[512,1152]{1,0:T(8,128)(2,1...) custom-call(s32[1]{0:T(128)} %bitcast.place_ref, ...), custom_call_target="tpu_custom_call" | custom-call | flops 61599997952 | bytes 62914560 | tf_op jit(solution)/shard_map/backward_blocks/pallas_call | solution.py:754
  278.9 3.5 add_convert_fusion.4
  282.4 12.8 %convolution_convert_fusion.1 = bf16[2048,1536]{1,0:T(8,128)(2,1)} fusion(bf16[2048,1152]{1,0:T(8,128)(2,1)} %get-tuple-element.216, bf16[1536,1152]{1,0:T(8,128)(2,1)S(1)} %copy-done.5), kind=kOutput, calls=%fused_computation.1 | convolution fusion | flops 7250903040 | bytes 14548992 | tf_op jit(solution)/shard_map/tf,df->td/dot_general | solution.py:959
  295.2 1.3 collective-permute-start.22
  297.0 20.6 %convolution_convert_fusion = bf16[1536,1152]{1,0:T(8,128)(2,1)} fusion(bf16[4096,1536]{1,0:T(8,128)(2,1)} %get-tuple-element.193, bf16[4096,1152]{1,0:T(8,128)(2,1)S(1)} %copy-done.42), kind=kOutput, calls=%fused_computation | convolution fusion | flops 14497284096 | bytes 25559040 | tf_op jit(solution)/shard_map/td,tf->df/dot_general | solution.py:962
  317.9 5.2 %fusion.14 = bf16[512,1536]{1,0:T(8,128)(2,1)} fusion(bf16[512,1152]{1,0:T(8,128)(2,1)} %get-tuple-element.234, bf16[1536,1152]{1,0:T(8,128)(2,1)S(1)} %copy-done.5, bf16[2048,1536]{1,0:T(8,128)(2,1)} %collective-permute-done.24), kind=kOutput, calls=%fused_computation.31 | convolution fusion | flops 1814298624 | bytes 7864320 | tf_op jit(solution)/shard_map/tf,df->td/dot_general | solution.py:959
  323.2 5.4 %fusion.13 = bf16[512,1536]{1,0:T(8,128)(2,1)} fusion(bf16[512,1152]{1,0:T(8,128)(2,1)S(1)} %copy-done.41, bf16[1536,1152]{1,0:T(8,128)(2,1)S(1)} %copy-done.5, bf16[2048,1536]{1,0:T(8,128)(2,1)} %collective-permute-done.24), kind=kOutput, calls=%fused_computation.30 | convolution fusion | flops 1814298624 | bytes 7864320 | tf_op jit(solution)/shard_map/tf,df->td/dot_general | solution.py:959
  328.5 6.1 %add_convert_fusion = bf16[1024,1536]{1,0:T(8,128)(2,1)S(1)} fusion(bf16[1024,1152]{1,0:T(8,128)(2,1)S(1)} %copy-done.43, bf16[1536,1152]{1,0:T(8,128)(2,1)S(1)} %copy-done.6, bf16[2048,1536]{1,0:T(8,128)(2,1)} %collective-permute-done.24), kind=kOutput, calls=%fused_computation.4 | convolution fusion | flops 3628597248 | bytes 12189696 | tf_op jit(solution)/shard_map/tf,df->td/dot_general | solution.py:959
  334.7 1.3 collective-permute-start.25
  336.5 1.0 multiply_reduce_fusion
  339.4 1.8 collective-permute-start.28
  341.2 40.1 %collective-permute-done.25 = bf16[512,1536]{1,0:T(8,128)(2,1)} collective-permute-done((bf16[512,1536]{1,0:T(8,128)(2,1)}, bf16[512,1536]{1,0:T(8,128)(2,1)}, u32[]{:S(2)}, u32[]{:S(2)}) %collective-permute-start.25) | collective-permute-done | bytes 1572896 | tf_op jit(solution)/shard_map/ppermute | solution.py:24
  381.4 2.9 add_convert_fusion.2
  384.3 4.3 collective-permute-start.30
  388.7 2.0 collective-permute-start.31
  390.6 23.7 %collective-permute-done.31 = f32[168,128]{1,0:T(8,128)S(1)} collective-permute-done((f32[168,128]{1,0:T(8,128)S(1)}, f32[168,128]{1,0:T(8,128)S(1)}, u32[]{:S(2)}, u32[]{:S(2)}) %collective-permute-start.31) | collective-permute-done | bytes 86048 | tf_op jit(solution)/shard_map/ppermute | solution.py:24
  414.5 3.1 add_bitcast_fusion.1
  417.6 1.8 collective-permute-start.33
  419.7 1.9 convert_add_fusion.2
  423.7 3.9 collective-permute-done.34
  427.6 7.9 %collective-permute-start.35 = (f32[168,128]{1,0:T(8,128)S(1)}, f32[168,128]{1,0:T(8,128)S(1)}, u32[]{:S(2)}, u32[]{:S(2)}) collective-permute-start(f32[168,128]{1,0:T(8,128)S(1)} %add.209), channel_id=1, source_target_pairs={{0,16},{8,24},{16,0},{24,8},{1,17},{9,25},{17,1},{25,9},{2,18},{10... | collective-permute-start | bytes 258056 | tf_op jit(solution)/shard_map/ppermute | solution.py:24
  435.5 4.6 collective-permute-done.36
  440.3 3.4 fusion.8
  445.1 1.5 reshape.221
  446.5 1.4 fusion.29
  447.9 1.3 slice_bitcast_fusion.3
  449.2 1.3 slice_bitcast_fusion.2
  450.5 1.6 pad_maximum_fusion.piece_ref
  452.2 6.2 %assemble_out_weight_grad.1 = f32[768,1536]{1,0:T(8,128)} custom-call(s32[1]{0:T(128)} %bitcast.place_ref, bf16[8,96,1536]{2,1,0:T(8,128)(2,1)} %pad_maximum_fusion.piece_ref), custom_call_target="tpu_custom_call" | custom-call | flops 5500000256 | bytes 7077888 | tf_op jit(solution)/shard_map/assemble_out_weight_grad/pallas_call | solution.py:810
  458.4 17.6 %all-gather.6.cloned.1.call-done = bf16[3072,1152]{1,0:T(8,128)(2,1)} async-done(((bf16[384,1152]{1,0:T(8,128)(2,1)}), bf16[3072,1152]{1,0:T(8,128)(2,1)}) %all-gather.6.cloned.1.call-update) | async-done | bytes 7077904 | tf_op jit(solution)/shard_map/all_gather | solution.py:1012
  476.0 8.2 %assemble_in_weight_grad.1 = f32[6448,384]{1,0:T(8,128)} custom-call(bf16[8,384,1152]{2,1,0:T(8,128)(2,1)} %bitcast.82), custom_call_target="tpu_custom_call" | custom-call | flops 8800000000 | bytes 14856192 | tf_op jit(solution)/shard_map/assemble_in_weight_grad/pallas_call | solution.py:844
  (235 shorter events, 21.8 us)
Async XLA Ops:
  7.2 88.2 %all-gather.4.cloned.1.call-start = ((), (), s32[]{:S(2)}) async-start(), calls=%async_computation.2 | async-start | bytes 4423680 | tf_op jit(solution)/shard_map/all_gather | solution.py:900
  11.8 149.4 %all-reduce.6.cloned.1.call-start = ((), (), s32[]{:S(2)}) async-start(), calls=%async_computation.3 | async-start | bytes 2359296 | tf_op jit(solution)/shard_map/psum | solution.py:192
  14.4 20.5 %collective-permute-start = (bf16[256,1536]{1,0:T(8,128)(2,1)S(1)}, bf16[256,1536]{1,0:T(8,128)(2,1)S(1)}, u32[]{:S(2)}, u32[]{:S(2)}) collective-permute-start(bf16[256,1536]{1,0:T(8,128)(2,1)S(1)} %get-tuple-element.286), channel_id=1, source_target_pairs={{0,2},{1,3},{2,0},{3,1},{4,6},{5,7},{6,4},{7,5},{8,10},{9,11},{10,... | collective-permute-start | bytes 2359304 | tf_op jit(solution)/shard_map/ppermute | solution.py:24
  17.4 19.6 %collective-permute-start.3 = (bf16[256,1536]{1,0:T(8,128)(2,1)S(1)}, bf16[256,1536]{1,0:T(8,128)(2,1)S(1)}, u32[]{:S(2)}, u32[]{:S(2)}) collective-permute-start(bf16[256,1536]{1,0:T(8,128)(2,1)S(1)} %get-tuple-element.285), channel_id=1, source_target_pairs={{0,4},{1,5},{2,6},{3,7},{4,0},{5,1},{6,2},{7,3},{8,12},{9,13},{10,... | collective-permute-start | bytes 2359304 | tf_op jit(solution)/shard_map/ppermute | solution.py:24
  35.1 3.9 collective-permute-start.2
  35.2 36.9 %collective-permute-start.1 = (bf16[512,1536]{1,0:T(8,128)(2,1)S(1)}, bf16[512,1536]{1,0:T(8,128)(2,1)}, u32[]{:S(2)}, u32[]{:S(2)}) collective-permute-start(bf16[512,1536]{1,0:T(8,128)(2,1)S(1)} %pad_maximum_fusion.1.refs_0_), channel_id=1, source_target_pairs={{0,4},{1,5},{2,6},{3,7},{4,0},{5,1},{6,2},{7,3},{8,12},{9,13},{10,... | collective-permute-start | bytes 4718600 | tf_op jit(solution)/shard_map/ppermute | solution.py:24
  37.1 35.0 %copy-start.10 = (bf16[512,1536]{1,0:T(8,128)(2,1)}, bf16[512,1536]{1,0:T(8,128)(2,1)S(1)}, u32[]{:S(2)}) copy-start(bf16[512,1536]{1,0:T(8,128)(2,1)S(1)} %pad_maximum_fusion.2.refs_4_) | copy-start | bytes 4718596
  37.1 39.9 %copy-start.36 = (f32[48]{0:T(128)S(1)}, f32[48]{0:T(128)}, u32[]{:S(2)}) copy-start(f32[48]{0:T(128)} %param.18) | copy-start | bytes 580
  37.1 40.0 %copy-start.27 = (f32[48]{0:T(128)S(1)}, f32[48]{0:T(128)}, u32[]{:S(2)}) copy-start(f32[48]{0:T(128)} %param.17) | copy-start | bytes 580
  37.1 40.0 %copy-start.28 = (f32[48]{0:T(128)S(1)}, f32[48]{0:T(128)}, u32[]{:S(2)}) copy-start(f32[48]{0:T(128)} %param.16) | copy-start | bytes 580
  37.1 40.9 %copy-start.23 = (f32[3328]{0:T(1024)S(1)}, f32[3328]{0:T(1024)}, u32[]{:S(2)}) copy-start(f32[3328]{0:T(1024)} %param.15) | copy-start | bytes 39940
  37.2 41.0 %slice-start.1 = ((f32[3328]{0:T(1024)}), f32[256]{0:T(256)S(1)}, s32[]{:S(2)}) async-start(f32[3328]{0:T(1024)} %param.15), calls=%async_computation.8 | async-start | bytes 2048 | tf_op jit(solution)/shard_map/slice | solution.py:885
  37.2 41.8 %copy-start.19 = (f32[4,3328]{1,0:T(4,128)S(1)}, f32[4,3328]{1,0:T(4,128)}, u32[]{:S(2)}) copy-start(f32[4,3328]{1,0:T(4,128)} %param.14) | copy-start | bytes 159748
  37.2 41.8 %slice-start = ((f32[4,3328]{1,0:T(4,128)}), f32[4,256]{1,0:T(4,128)S(1)}, s32[]{:S(2)}) async-start(f32[4,3328]{1,0:T(4,128)} %param.14), calls=%async_computation.7 | async-start | bytes 8192 | tf_op jit(solution)/shard_map/slice | solution.py:885
  37.2 34.9 %collective-permute-start.5 = (bf16[512,1536]{1,0:T(8,128)(2,1)S(1)}, bf16[512,1536]{1,0:T(8,128)(2,1)S(1)}, u32[]{:S(2)}, u32[]{:S(2)}) collective-permute-start(bf16[512,1536]{1,0:T(8,128)(2,1)S(1)} %pad_maximum_fusion.2.refs_4_), channel_id=1, source_target_pairs={{0,1},{1,0},{2,3},{3,2},{4,5},{5,4},{6,7},{7,6},{8,9},{9,8},{10,11... | collective-permute-start | bytes 4718600 | tf_op jit(solution)/shard_map/ppermute | solution.py:24
  37.4 36.7 %collective-permute-start.4 = (bf16[512,1536]{1,0:T(8,128)(2,1)S(1)}, bf16[512,1536]{1,0:T(8,128)(2,1)}, u32[]{:S(2)}, u32[]{:S(2)}) collective-permute-start(bf16[512,1536]{1,0:T(8,128)(2,1)S(1)} %pad_maximum_fusion.2.refs_4_), channel_id=1, source_target_pairs={{0,2},{1,3},{2,0},{3,1},{4,6},{5,7},{6,4},{7,5},{8,10},{9,11},{10,... | collective-permute-start | bytes 4718600 | tf_op jit(solution)/shard_map/ppermute | solution.py:24
  39.0 35.7 %copy-start.29 = (bf16[512,1536]{1,0:T(8,128)(2,1)}, bf16[512,1536]{1,0:T(8,128)(2,1)S(1)}, u32[]{:S(2)}) copy-start(bf16[512,1536]{1,0:T(8,128)(2,1)S(1)} %collective-permute-done.2.refs_2_) | copy-start | bytes 4718596
  74.2 21.2 %collective-permute-start.6 = (bf16[512,1536]{1,0:T(8,128)(2,1)}, bf16[512,1536]{1,0:T(8,128)(2,1)}, u32[]{:S(2)}, u32[]{:S(2)}) collective-permute-start(bf16[512,1536]{1,0:T(8,128)(2,1)} %collective-permute-done.1.refs_1_), channel_id=1, source_target_pairs={{0,1},{1,0},{2,3},{3,2},{4,5},{5,4},{6,7},{7,6},{8,9},{9,8},{10,11... | collective-permute-start | bytes 4718600 | tf_op jit(solution)/shard_map/ppermute | solution.py:24
  74.2 21.2 %collective-permute-start.7 = (bf16[512,1536]{1,0:T(8,128)(2,1)}, bf16[512,1536]{1,0:T(8,128)(2,1)}, u32[]{:S(2)}, u32[]{:S(2)}) collective-permute-start(bf16[512,1536]{1,0:T(8,128)(2,1)} %collective-permute-done.4.refs_5_), channel_id=1, source_target_pairs={{0,1},{1,0},{2,3},{3,2},{4,5},{5,4},{6,7},{7,6},{8,9},{9,8},{10,11... | collective-permute-start | bytes 4718600 | tf_op jit(solution)/shard_map/ppermute | solution.py:24
  74.7 19.4 %collective-permute-start.8 = (bf16[256,1536]{1,0:T(8,128)(2,1)S(1)}, bf16[256,1536]{1,0:T(8,128)(2,1)S(1)}, u32[]{:S(2)}, u32[]{:S(2)}) collective-permute-start(bf16[256,1536]{1,0:T(8,128)(2,1)S(1)} %get-tuple-element.162), channel_id=1, source_target_pairs={{0,2},{1,3},{2,0},{3,1},{4,6},{5,7},{6,4},{7,5},{8,10},{9,11},{10,... | collective-permute-start | bytes 2359304 | tf_op jit(solution)/shard_map/ppermute | solution.py:24
  76.2 19.2 %collective-permute-start.9 = (bf16[256,1536]{1,0:T(8,128)(2,1)S(1)}, bf16[256,1536]{1,0:T(8,128)(2,1)S(1)}, u32[]{:S(2)}, u32[]{:S(2)}) collective-permute-start(bf16[256,1536]{1,0:T(8,128)(2,1)S(1)} %get-tuple-element.164), channel_id=1, source_target_pairs={{0,4},{1,5},{2,6},{3,7},{4,0},{5,1},{6,2},{7,3},{8,12},{9,13},{10,... | collective-permute-start | bytes 2359304 | tf_op jit(solution)/shard_map/ppermute | solution.py:24
  97.2 64.0 %collective-permute-start.13 = (bf16[512,1536]{1,0:T(8,128)(2,1)}, bf16[512,1536]{1,0:T(8,128)(2,1)}, u32[]{:S(2)}, u32[]{:S(2)}) collective-permute-start(bf16[512,1536]{1,0:T(8,128)(2,1)} %constant_dynamic-update-slice_fusion.2.refs_4_), channel_id=1, source_target_pairs={{0,1},{1,0},{2,3},{3,2},{4,5},{5,4},{6,7},{7,6},{8,9},{9,8},{10,11... | collective-permute-start | bytes 4718600 | tf_op jit(solution)/shard_map/ppermute | solution.py:24
  97.2 64.0 %collective-permute-start.12 = (bf16[512,1536]{1,0:T(8,128)(2,1)}, bf16[512,1536]{1,0:T(8,128)(2,1)}, u32[]{:S(2)}, u32[]{:S(2)}) collective-permute-start(bf16[512,1536]{1,0:T(8,128)(2,1)} %constant_dynamic-update-slice_fusion.2.refs_4_), channel_id=1, source_target_pairs={{0,2},{1,3},{2,0},{3,1},{4,6},{5,7},{6,4},{7,5},{8,10},{9,11},{10,... | collective-permute-start | bytes 4718600 | tf_op jit(solution)/shard_map/ppermute | solution.py:24
  99.8 61.5 %collective-permute-start.11 = (bf16[512,1536]{1,0:T(8,128)(2,1)}, bf16[512,1536]{1,0:T(8,128)(2,1)S(1)}, u32[]{:S(2)}, u32[]{:S(2)}) collective-permute-start(bf16[512,1536]{1,0:T(8,128)(2,1)} %constant_dynamic-update-slice_fusion.refs_0_), channel_id=1, source_target_pairs={{0,1},{1,0},{2,3},{3,2},{4,5},{5,4},{6,7},{7,6},{8,9},{9,8},{10,11... | collective-permute-start | bytes 4718600 | tf_op jit(solution)/shard_map/ppermute | solution.py:24
  100.0 61.3 %collective-permute-start.10 = (bf16[512,1536]{1,0:T(8,128)(2,1)}, bf16[512,1536]{1,0:T(8,128)(2,1)S(1)}, u32[]{:S(2)}, u32[]{:S(2)}) collective-permute-start(bf16[512,1536]{1,0:T(8,128)(2,1)} %constant_dynamic-update-slice_fusion.refs_0_), channel_id=1, source_target_pairs={{0,4},{1,5},{2,6},{3,7},{4,0},{5,1},{6,2},{7,3},{8,12},{9,13},{10,... | collective-permute-start | bytes 4718600 | tf_op jit(solution)/shard_map/ppermute | solution.py:24
  102.2 180.1 %reduce-scatter.3.cloned.1.call-start = ((), (), s32[]{:S(2)}) async-start(), calls=%async_computation.4 | async-start | bytes 1474560 | tf_op jit(solution)/shard_map/reduce_scatter | solution.py:948
  161.3 9.0 %copy-start.31 = (bf16[512,1536]{1,0:T(8,128)(2,1)}, bf16[512,1536]{1,0:T(8,128)(2,1)S(1)}, u32[]{:S(2)}) copy-start(bf16[512,1536]{1,0:T(8,128)(2,1)S(1)} %collective-permute-done.11.refs_2_) | copy-start | bytes 4718596
  161.3 9.0 %copy-start.32 = (bf16[512,1536]{1,0:T(8,128)(2,1)}, bf16[512,1536]{1,0:T(8,128)(2,1)S(1)}, u32[]{:S(2)}) copy-start(bf16[512,1536]{1,0:T(8,128)(2,1)S(1)} %collective-permute-done.10.refs_1_) | copy-start | bytes 4718596
  161.3 9.0 %collective-permute-start.14 = (bf16[512,1536]{1,0:T(8,128)(2,1)S(1)}, bf16[512,1536]{1,0:T(8,128)(2,1)S(1)}, u32[]{:S(2)}, u32[]{:S(2)}) collective-permute-start(bf16[512,1536]{1,0:T(8,128)(2,1)S(1)} %collective-permute-done.10.refs_1_), channel_id=1, source_target_pairs={{0,1},{1,0},{2,3},{3,2},{4,5},{5,4},{6,7},{7,6},{8,9},{9,8},{10,11... | collective-permute-start | bytes 4718600 | tf_op jit(solution)/shard_map/ppermute | solution.py:24
  161.4 8.9 %collective-permute-start.15 = (bf16[512,1536]{1,0:T(8,128)(2,1)}, bf16[512,1536]{1,0:T(8,128)(2,1)S(1)}, u32[]{:S(2)}, u32[]{:S(2)}) collective-permute-start(bf16[512,1536]{1,0:T(8,128)(2,1)} %collective-permute-done.12.refs_5_), channel_id=1, source_target_pairs={{0,1},{1,0},{2,3},{3,2},{4,5},{5,4},{6,7},{7,6},{8,9},{9,8},{10,11... | collective-permute-start | bytes 4718600 | tf_op jit(solution)/shard_map/ppermute | solution.py:24
  170.3 23.2 %collective-permute-start.17 = (bf16[2048,1536]{1,0:T(8,128)(2,1)}, bf16[2048,1536]{1,0:T(8,128)(2,1)}, u32[]{:S(2)}, u32[]{:S(2)}) collective-permute-start(bf16[2048,1536]{1,0:T(8,128)(2,1)} %convolution_convert_fusion.2), channel_id=1, source_target_pairs={{0,1},{1,0},{2,3},{3,2},{4,5},{5,4},{6,7},{7,6},{8,9},{9,8},{10,11... | collective-permute-start | bytes 18874376 | tf_op jit(solution)/shard_map/ppermute | solution.py:24
  172.8 20.7 %copy-start.35 = (bf16[384,1536]{1,0:T(8,128)(2,1)S(1)}, bf16[384,1536]{1,0:T(8,128)(2,1)}, u32[]{:S(2)}) copy-start(bf16[384,1536]{1,0:T(8,128)(2,1)} %all-reduce.6.cloned.1.call-done.refs_9_) | copy-start | bytes 3538948
  172.9 20.7 %copy-start.38 = (bf16[512,384]{1,0:T(8,128)(2,1)S(1)}, bf16[512,384]{1,0:T(8,128)(2,1)}, u32[]{:S(2)}) copy-start(bf16[512,384]{1,0:T(8,128)(2,1)} %get-tuple-element.187) | copy-start | bytes 1179652
  192.2 1.3 collective-permute-start.16
  193.5 19.2 %slice-start.2 = ((s8[12582912]{0:T(1024)(128)(4,1)}), s8[4194304]{0:T(1024)(128)(4,1)S(1)}, s32[]{:S(2)}) async-start(s8[12582912]{0:T(1024)(128)(4,1)} %bitcast.84), calls=%async_computation.9 | async-start | bytes 8388608
  197.2 8.8 %copy-start.40 = (bf16[1024,384]{1,0:T(8,128)(2,1)S(1)}, bf16[1024,384]{1,0:T(8,128)(2,1)}, u32[]{:S(2)}) copy-start(bf16[1024,384]{1,0:T(8,128)(2,1)} %get-tuple-element.212) | copy-start | bytes 2359300
  197.2 15.5 %slice-start.3 = ((s8[12582912]{0:T(1024)(128)(4,1)}), s8[4194304]{0:T(1024)(128)(4,1)S(1)}, s32[]{:S(2)}) async-start(s8[12582912]{0:T(1024)(128)(4,1)} %bitcast.84), calls=%async_computation.10 | async-start | bytes 8388608
  201.0 3.9 collective-permute-start.18
  204.9 7.1 %collective-permute-start.19 = (f32[2,4096]{1,0:T(2,128)S(1)}, f32[2,4096]{1,0:T(2,128)S(1)}, u32[]{:S(2)}, u32[]{:S(2)}) collective-permute-start(f32[2,4096]{1,0:T(2,128)S(1)} %add.183), channel_id=1, source_target_pairs={{0,4},{1,5},{2,6},{3,7},{4,0},{5,1},{6,2},{7,3},{8,12},{9,13},{10,... | collective-permute-start | bytes 98312 | tf_op jit(solution)/shard_map/ppermute | solution.py:24
  219.1 195.3 %reduce-scatter.5.cloned.1.call-start = ((), (), s32[]{:S(2)}) async-start(), calls=%async_computation.5 | async-start | bytes 4423680 | tf_op jit(solution)/shard_map/reduce_scatter | solution.py:970
  219.2 59.7 %collective-permute-start.20 = (bf16[512,1536]{1,0:T(8,128)(2,1)}, bf16[512,1536]{1,0:T(8,128)(2,1)}, u32[]{:S(2)}, u32[]{:S(2)}) collective-permute-start(bf16[512,1536]{1,0:T(8,128)(2,1)} %fusion.15), channel_id=1, source_target_pairs={{0,2},{1,3},{2,0},{3,1},{4,6},{5,7},{6,4},{7,5},{8,10},{9,11},{10,... | collective-permute-start | bytes 4718600 | tf_op jit(solution)/shard_map/ppermute | solution.py:24
  220.7 58.1 %collective-permute-start.21 = (bf16[512,1536]{1,0:T(8,128)(2,1)}, bf16[512,1536]{1,0:T(8,128)(2,1)}, u32[]{:S(2)}, u32[]{:S(2)}) collective-permute-start(bf16[512,1536]{1,0:T(8,128)(2,1)} %fusion.16), channel_id=1, source_target_pairs={{0,4},{1,5},{2,6},{3,7},{4,0},{5,1},{6,2},{7,3},{8,12},{9,13},{10,... | collective-permute-start | bytes 4718600 | tf_op jit(solution)/shard_map/ppermute | solution.py:24
  282.4 14.6 %copy-start.42 = (bf16[4096,1152]{1,0:T(8,128)(2,1)S(1)}, bf16[4096,1152]{1,0:T(8,128)(2,1)}, u32[]{:S(2)}) copy-start(bf16[4096,1152]{1,0:T(8,128)(2,1)} %get-tuple-element.218) | copy-start | bytes 28311556
  295.1 22.8 %collective-permute-start.24 = (bf16[2048,1536]{1,0:T(8,128)(2,1)}, bf16[2048,1536]{1,0:T(8,128)(2,1)}, u32[]{:S(2)}, u32[]{:S(2)}) collective-permute-start(bf16[2048,1536]{1,0:T(8,128)(2,1)} %convolution_convert_fusion.1), channel_id=1, source_target_pairs={{0,1},{1,0},{2,3},{3,2},{4,5},{5,4},{6,7},{7,6},{8,9},{9,8},{10,11... | collective-permute-start | bytes 18874376 | tf_op jit(solution)/shard_map/ppermute | solution.py:24
  295.2 22.5 %collective-permute-start.22 = (bf16[256,1536]{1,0:T(8,128)(2,1)}, bf16[256,1536]{1,0:T(8,128)(2,1)}, u32[]{:S(2)}, u32[]{:S(2)}) collective-permute-start(bf16[256,1536]{1,0:T(8,128)(2,1)} %get-tuple-element.223), channel_id=1, source_target_pairs={{0,4},{1,5},{2,6},{3,7},{4,0},{5,1},{6,2},{7,3},{8,12},{9,13},{10,... | collective-permute-start | bytes 2359304 | tf_op jit(solution)/shard_map/ppermute | solution.py:24
  296.4 21.2 %collective-permute-start.23 = (bf16[256,1536]{1,0:T(8,128)(2,1)}, bf16[256,1536]{1,0:T(8,128)(2,1)}, u32[]{:S(2)}, u32[]{:S(2)}) collective-permute-start(bf16[256,1536]{1,0:T(8,128)(2,1)} %get-tuple-element.225), channel_id=1, source_target_pairs={{0,2},{1,3},{2,0},{3,1},{4,6},{5,7},{6,4},{7,5},{8,10},{9,11},{10,... | collective-permute-start | bytes 2359304 | tf_op jit(solution)/shard_map/ppermute | solution.py:24
  317.6 158.4 %all-gather.6.cloned.1.call-start = ((), (), s32[]{:S(2)}) async-start(), calls=%async_computation.6 | async-start | bytes 7962624 | tf_op jit(solution)/shard_map/all_gather | solution.py:1012
  328.5 8.0 %copy-start.2 = (bf16[1536,1152]{1,0:T(8,128)(2,1)S(1)}, bf16[1536,1152]{1,0:T(8,128)(2,1)}, u32[]{:S(2)}) copy-start(bf16[1536,1152]{1,0:T(8,128)(2,1)} %convolution_convert_fusion) | copy-start | bytes 10616836
  334.6 46.8 %copy-start.7 = (bf16[1024,1536]{1,0:T(8,128)(2,1)}, bf16[1024,1536]{1,0:T(8,128)(2,1)S(1)}, u32[]{:S(2)}) copy-start(bf16[1024,1536]{1,0:T(8,128)(2,1)S(1)} %add_convert_fusion) | copy-start | bytes 9437188
  334.7 46.7 %collective-permute-start.25 = (bf16[512,1536]{1,0:T(8,128)(2,1)}, bf16[512,1536]{1,0:T(8,128)(2,1)}, u32[]{:S(2)}, u32[]{:S(2)}) collective-permute-start(bf16[512,1536]{1,0:T(8,128)(2,1)} %fusion.13), channel_id=1, source_target_pairs={{0,2},{1,3},{2,0},{3,1},{4,6},{5,7},{6,4},{7,5},{8,10},{9,11},{10,... | collective-permute-start | bytes 4718600 | tf_op jit(solution)/shard_map/ppermute | solution.py:24
  336.0 45.4 %collective-permute-start.26 = (bf16[512,1536]{1,0:T(8,128)(2,1)}, bf16[512,1536]{1,0:T(8,128)(2,1)}, u32[]{:S(2)}, u32[]{:S(2)}) collective-permute-start(bf16[512,1536]{1,0:T(8,128)(2,1)} %fusion.14), channel_id=1, source_target_pairs={{0,4},{1,5},{2,6},{3,7},{4,0},{5,1},{6,2},{7,3},{8,12},{9,13},{10,... | collective-permute-start | bytes 4718600 | tf_op jit(solution)/shard_map/ppermute | solution.py:24
  339.3 1.9 collective-permute-start.27
  339.4 44.9 %collective-permute-start.28 = (bf16[96,1536]{1,0:T(8,128)(2,1)}, bf16[96,1536]{1,0:T(8,128)(2,1)S(1)}, u32[]{:S(2)}, u32[]{:S(2)}) collective-permute-start(bf16[96,1536]{1,0:T(8,128)(2,1)} %reduce-scatter.3.cloned.1.call-done), channel_id=1, source_target_pairs={{0,0},{1,1},{8,2},{9,3},{16,4},{17,5},{24,6},{25,7},{2,8},{3,9},{1... | collective-permute-start | bytes 884744 | tf_op jit(solution)/shard_map/ppermute | solution.py:196
  384.3 30.2 %collective-permute-start.29 = (bf16[256,1536]{1,0:T(8,128)(2,1)}, bf16[256,1536]{1,0:T(8,128)(2,1)S(1)}, u32[]{:S(2)}, u32[]{:S(2)}) collective-permute-start(bf16[256,1536]{1,0:T(8,128)(2,1)} %get-tuple-element.258), channel_id=1, source_target_pairs={{0,4},{1,5},{2,6},{3,7},{4,0},{5,1},{6,2},{7,3},{8,12},{9,13},{10,... | collective-permute-start | bytes 2359304 | tf_op jit(solution)/shard_map/ppermute | solution.py:24
  384.3 30.2 %collective-permute-start.30 = (bf16[256,1536]{1,0:T(8,128)(2,1)}, bf16[256,1536]{1,0:T(8,128)(2,1)S(1)}, u32[]{:S(2)}, u32[]{:S(2)}) collective-permute-start(bf16[256,1536]{1,0:T(8,128)(2,1)} %get-tuple-element.259), channel_id=1, source_target_pairs={{0,2},{1,3},{2,0},{3,1},{4,6},{5,7},{6,4},{7,5},{8,10},{9,11},{10,... | collective-permute-start | bytes 2359304 | tf_op jit(solution)/shard_map/ppermute | solution.py:24
  388.6 25.7 %collective-permute-start.32 = (bf16[1,96,1536]{2,1,0:T(8,128)(2,1)S(1)}, bf16[1,96,1536]{2,1,0:T(8,128)(2,1)S(1)}, u32[]{:S(2)}, u32[]{:S(2)}) collective-permute-start(bf16[1,96,1536]{2,1,0:T(8,128)(2,1)S(1)} %bitcast.73), channel_id=1, source_target_pairs={{0,2},{1,3},{2,0},{3,1},{4,6},{5,7},{6,4},{7,5},{8,10},{9,11},{10,... | collective-permute-start | bytes 884744 | tf_op jit(solution)/shard_map/ppermute | solution.py:24
  388.7 25.7 %collective-permute-start.31 = (f32[168,128]{1,0:T(8,128)S(1)}, f32[168,128]{1,0:T(8,128)S(1)}, u32[]{:S(2)}, u32[]{:S(2)}) collective-permute-start(f32[168,128]{1,0:T(8,128)S(1)} %fusion.25), channel_id=1, source_target_pairs={{0,2},{1,3},{2,0},{3,1},{4,6},{5,7},{6,4},{7,5},{8,10},{9,11},{10,... | collective-permute-start | bytes 258056 | tf_op jit(solution)/shard_map/ppermute | solution.py:24
  417.6 5.4 %collective-permute-start.33 = (f32[168,128]{1,0:T(8,128)S(1)}, f32[168,128]{1,0:T(8,128)S(1)}, u32[]{:S(2)}, u32[]{:S(2)}) collective-permute-start(f32[168,128]{1,0:T(8,128)S(1)} %add.202), channel_id=1, source_target_pairs={{0,4},{1,5},{2,6},{3,7},{4,0},{5,1},{6,2},{7,3},{8,12},{9,13},{10,... | collective-permute-start | bytes 258056 | tf_op jit(solution)/shard_map/ppermute | solution.py:24
  419.4 20.7 %collective-permute-start.36 = (bf16[2,96,1536]{2,1,0:T(8,128)(2,1)S(1)}, bf16[2,96,1536]{2,1,0:T(8,128)(2,1)S(1)}, u32[]{:S(2)}, u32[]{:S(2)}) collective-permute-start(bf16[2,96,1536]{2,1,0:T(8,128)(2,1)S(1)} %pad_maximum_fusion.4), channel_id=1, source_target_pairs={{0,4},{1,5},{2,6},{3,7},{4,0},{5,1},{6,2},{7,3},{8,12},{9,13},{10,... | collective-permute-start | bytes 1769480 | tf_op jit(solution)/shard_map/ppermute | solution.py:24
  422.1 18.2 %copy-start.4 = (bf16[1,512,1536]{2,1,0:T(8,128)(2,1)S(1)}, bf16[1,512,1536]{2,1,0:T(8,128)(2,1)}, u32[]{:S(2)}) copy-start(bf16[1,512,1536]{2,1,0:T(8,128)(2,1)} %param.21) | copy-start | bytes 4718596
  422.1 18.2 %copy-start.18 = (f32[512]{0:T(512)S(1)}, f32[512]{0:T(512)}, u32[]{:S(2)}) copy-start(f32[512]{0:T(512)} %copy-done.17) | copy-start | bytes 6148
  423.0 4.6 collective-permute-start.34
  427.6 16.1 %collective-permute-start.35 = (f32[168,128]{1,0:T(8,128)S(1)}, f32[168,128]{1,0:T(8,128)S(1)}, u32[]{:S(2)}, u32[]{:S(2)}) collective-permute-start(f32[168,128]{1,0:T(8,128)S(1)} %add.209), channel_id=1, source_target_pairs={{0,16},{8,24},{16,0},{24,8},{1,17},{9,25},{17,1},{25,9},{2,18},{10... | collective-permute-start | bytes 258056 | tf_op jit(solution)/shard_map/ppermute | solution.py:24
  440.2 10.3 %collective-permute-start.37 = (bf16[4,96,1536]{2,1,0:T(8,128)(2,1)S(1)}, bf16[4,96,1536]{2,1,0:T(8,128)(2,1)S(1)}, u32[]{:S(2)}, u32[]{:S(2)}) collective-permute-start(bf16[4,96,1536]{2,1,0:T(8,128)(2,1)S(1)} %pad_maximum_fusion.3), channel_id=1, source_target_pairs={{0,1},{1,0},{2,3},{3,2},{4,5},{5,4},{6,7},{7,6},{8,9},{9,8},{10,11... | collective-permute-start | bytes 3538952 | tf_op jit(solution)/shard_map/ppermute | solution.py:24
  (28 other events, 94.5 us)
Sparse Core Ops, SparseCore 0:
  12.0 72.6 all-gather.3
  102.4 56.6 all-reduce.5
  219.2 29.6 reduce-scatter.2
  317.8 85.5 reduce-scatter.4
  414.6 61.3 all-gather.5

commit v2 on v1

--- a/solution.py
+++ b/solution.py
@@ -1006,9 +1006,10 @@
         back_ready, back_held = scatter_far(back_ready, back_held, stage)
     out_pieces = double(out_pieces, 0)
     vector = vector + exchange(vector, *axes.pop(0))
-    back_held["arrived"], vector, out_pieces, in_sum = together(
-        back_held["arrived"], vector, out_pieces, in_sum
-    )
+    first_half, vector, out_pieces, in_sum = together(
+        back_held["arrived"][0], vector, out_pieces, in_sum
+    )
+    back_held["arrived"] = (first_half, back_held["arrived"][1])
     pieces = lax.all_gather(in_sum, "seq", axis=0, tiled=False)
     in_weight_grad = assemble(pieces, dims).T
     for stage in range(1, stages):

time: 500 us -> 491 us (0.982)
  waiting for transfers between devices: 161 us -> 149 us
    all_gather x1, waiting for transfers between devices: 17.6 us -> 2.1 us  [body(): pieces = lax.all_gather(in_sum, 'seq', axis=0, tiled=False)]
    reduce_scatter x1, waiting for transfers between devices: 0.02 us -> 5.96 us  [body(): in_sum = lax.psum_scatter(in_term, 'batch', scatter_dimension=0, tiled=True)]
where the time goes in v2:
time: 491 us; the launch traced here: 483 us
  waiting for transfers between devices  149 us (30%)
  Pallas kernels  148 us (30%)
  matrix products  78.1 us (16%)
  starting transfers between devices  44.5 us (9%)
  other arithmetic  24.1 us (5%)
  local copies, waits for them, and re-layouts  23.3 us (5%)
  between operations  14.9 us (3%)
    ppermute x37, waiting for transfers between devices, exchange(): lax.ppermute(value, axis, [(source, source ^ distance) for source in rang...  141 us
    pallas_call x1, Pallas kernels, run_forward(): pl.pallas_call(functools.partial(forward_kernel, dims, table, len(arrays)...  58.3 us
    pallas_call x1, Pallas kernels, run_backward(): pl.pallas_call(functools.partial(backward_kernel, dims), grid_spec=pltpu....  57.4 us
    ppermute x37, starting transfers between devices, exchange(): lax.ppermute(value, axis, [(source, source ^ distance) for source in rang...  42.2 us
    dot_general x4, matrix products, back_product(): return jnp.einsum('tf,df->td', part, w_cols, preferred_element_type=f32)  29.4 us
    dot_general x4, matrix products, dot(): return jnp.dot(a, b, preferred_element_type=f32)  21.7 us
    dot_general x1, matrix products, weight_product(): jnp.einsum('td,tf->df', normed, part, preferred_element_type=f32)  20.6 us
    pallas_call x1, Pallas kernels, run_out_grad(): pl.pallas_call(functools.partial(out_grad_kernel, table, len(arrays)), gr...  18.3 us
  transfers between devices with their start and end apart: 43, of which 13 were waited for; matrix products, arithmetic and copies ran while one was open for 18% of the time, Pallas kernels for 29%

profile of v2, /device:TPU:0, one launch (start us, length us, event | category | flops | bytes accessed | tf_op | source)
XLA Modules:
  0.0 482.7 jit_solution(12254816460366681991)
XLA Ops:
  7.2 1.0 slice.151
  9.2 1.1 constant_dynamic-slice_fusion.4
  10.8 1.0 fusion.19
  14.4 3.0 collective-permute-start
  17.4 1.5 collective-permute-start.3
  18.9 16.0 %collective-permute-done = bf16[256,1536]{1,0:T(8,128)(2,1)S(1)} collective-permute-done((bf16[256,1536]{1,0:T(8,128)(2,1)S(1)}, bf16[256,1536]{1,0:T(8,128)(2,1)S(1)}, u32[]{:S(2)}, u32[]{:S(2)}) %collective-permute-start) | collective-permute-done | bytes 786464 | tf_op jit(solution)/shard_map/ppermute | solution.py:24
  35.2 1.8 collective-permute-start.1
  37.4 1.5 collective-permute-start.4
  39.0 33.0 %collective-permute-done.1.refs_1_ = bf16[512,1536]{1,0:T(8,128)(2,1)} collective-permute-done((bf16[512,1536]{1,0:T(8,128)(2,1)S(1)}, bf16[512,1536]{1,0:T(8,128)(2,1)}, u32[]{:S(2)}, u32[]{:S(2)}) %collective-permute-start.1) | collective-permute-done | bytes 1572896 | tf_op jit(solution)/shard_map/ppermute | solution.py:24
  72.1 2.1 collective-permute-done.4.refs_5_
  74.7 1.5 collective-permute-start.8
  80.2 13.9 %collective-permute-done.8 = bf16[256,1536]{1,0:T(8,128)(2,1)S(1)} collective-permute-done((bf16[256,1536]{1,0:T(8,128)(2,1)S(1)}, bf16[256,1536]{1,0:T(8,128)(2,1)S(1)}, u32[]{:S(2)}, u32[]{:S(2)}) %collective-permute-start.8) | collective-permute-done | bytes 786464 | tf_op jit(solution)/shard_map/ppermute | solution.py:24
  94.1 1.2 collective-permute-done.9
  95.4 1.0 constant_dynamic-update-slice_fusion.3
  96.3 0.9 constant_dynamic-update-slice_fusion.2.refs_4_
  97.8 1.0 constant_dynamic-update-slice_fusion.1
  98.8 1.0 constant_dynamic-update-slice_fusion.refs_0_
  100.0 0.9 collective-permute-start.10
  100.9 1.3 dynamic-slice_select_fusion
  103.0 58.3 %forward_blocks.1 = (bf16[4096,640]{1,0:T(8,128)(2,1)}, bf16[4096,640]{1,0:T(8,128)(2,1)}, bf16[4096,640]{1,0:T(8,128)(2,1)}, bf16[4096,384]{1,0:T(8,128)(2,1)},...) custom-call(s32[1]{0:T(128)} %bitcast.place_ref, ...), custom_call_target="tpu_custom_call" | custom-call | flops 52800000000 | bytes 62914560 | tf_op jit(solution)/shard_map/forward_blocks/pallas_call | solution.py:470
  161.9 8.4 %convolution_convert_fusion.2 = bf16[2048,1536]{1,0:T(8,128)(2,1)} fusion(bf16[2048,384]{1,0:T(8,128)(2,1)} %get-tuple-element.165, bf16[384,1536]{1,0:T(8,128)(2,1)} %all-reduce.6.cloned.1.call-done.refs_9_), kind=kOutput, calls=%fused_computation.2 | convolution fusion | flops 2419064832 | bytes 9043968 | tf_op jit(solution)/shard_map/dot_general | solution.py:217
  170.4 1.0 copy-done.34
  172.8 18.3 %out_grad.1 = (f32[4096,384]{1,0:T(8,128)}, f32[16,8,256]{2,1,0:T(8,128)}, bf16[4096,1536]{1,0:T(8,128)(2,1)}) custom-call(s32[1]{0:T(128)} %bitcast.place_ref, bf16[512,1536]{1,0:T(8,128)(2,1)} %constant_dynamic-update-slice_fusion.refs_0_, bf16[512,1536]{1,0:T(8,128)(2,1)} %copy-done.33, bf16[512,1536]{1,0:T(8,128)(2,1)} %copy-done.32, ...), custom_call_target="tpu_custom_call" | custom-call | flops 13200000000 | bytes 34603008 | tf_op jit(solution)/shard_map/out_grad/pallas_call | solution.py:555
  192.3 1.2 collective-permute-done.16
  193.5 3.7 fusion.16
  197.2 3.7 fusion.15
  201.0 1.4 collective-permute-start.18
  202.3 2.5 collective-permute-done.18
  204.9 1.2 collective-permute-start.19
  206.1 5.9 %add_convert_fusion.1 = bf16[1024,1536]{1,0:T(8,128)(2,1)} fusion(bf16[1024,384]{1,0:T(8,128)(2,1)S(1)} %copy-done.41, bf16[384,1536]{1,0:T(8,128)(2,1)S(1)} %copy-done.36, bf16[2048,1536]{1,0:T(8,128)(2,1)} %collective-permute-done.17), kind=kOutput, calls=%fused_computation.5 | convolution fusion | flops 1212678144 | bytes 8257536 | tf_op jit(solution)/shard_map/dot_general | solution.py:217
  212.8 6.3 %fusion.17 = bf16[384,1536]{1,0:T(8,128)(2,1)} fusion(bf16[4096,1536]{1,0:T(8,128)(2,1)S(1)} %bitcast.85, bf16[4096,384]{1,0:T(8,128)(2,1)S(1)} %copy-done.40, f32[4096]{0:T(1024)S(1)} %bitcast.80), kind=kOutput, calls=%fused_computation.34 | convolution fusion | flops 4837146624 | bytes 16924672 | tf_op jit(solution)/shard_map/te,td->ed/dot_general | solution.py:946
  219.2 1.6 collective-permute-start.20
  221.5 57.4 %backward_blocks.1 = (bf16[4096,1152]{1,0:T(8,128)(2,1)}, bf16[2048,1152]{1,0:T(8,128)(2,1)}, bf16[512,1152]{1,0:T(8,128)(2,1)}, bf16[512,1152]{1,0:T(8,128)(2,1...) custom-call(s32[1]{0:T(128)} %bitcast.place_ref, ...), custom_call_target="tpu_custom_call" | custom-call | flops 61599997952 | bytes 62914560 | tf_op jit(solution)/shard_map/backward_blocks/pallas_call | solution.py:754
  278.9 3.5 add_convert_fusion.4
  282.4 12.8 %convolution_convert_fusion.1 = bf16[2048,1536]{1,0:T(8,128)(2,1)} fusion(bf16[2048,1152]{1,0:T(8,128)(2,1)} %get-tuple-element.214, bf16[1536,1152]{1,0:T(8,128)(2,1)S(1)} %copy-done.5), kind=kOutput, calls=%fused_computation.1 | convolution fusion | flops 7250903040 | bytes 14548992 | tf_op jit(solution)/shard_map/tf,df->td/dot_general | solution.py:959
  295.2 1.4 collective-permute-start.22
  297.0 20.6 %convolution_convert_fusion = bf16[1536,1152]{1,0:T(8,128)(2,1)} fusion(bf16[4096,1536]{1,0:T(8,128)(2,1)} %get-tuple-element.191, bf16[4096,1152]{1,0:T(8,128)(2,1)S(1)} %copy-done.43), kind=kOutput, calls=%fused_computation | convolution fusion | flops 14497284096 | bytes 25559040 | tf_op jit(solution)/shard_map/td,tf->df/dot_general | solution.py:962
  318.0 5.2 %fusion.14 = bf16[512,1536]{1,0:T(8,128)(2,1)} fusion(bf16[512,1152]{1,0:T(8,128)(2,1)} %get-tuple-element.232, bf16[1536,1152]{1,0:T(8,128)(2,1)S(1)} %copy-done.5, bf16[2048,1536]{1,0:T(8,128)(2,1)} %collective-permute-done.24), kind=kOutput, calls=%fused_computation.31 | convolution fusion | flops 1814298624 | bytes 7864320 | tf_op jit(solution)/shard_map/tf,df->td/dot_general | solution.py:959
  323.2 5.4 %fusion.13 = bf16[512,1536]{1,0:T(8,128)(2,1)} fusion(bf16[512,1152]{1,0:T(8,128)(2,1)S(1)} %copy-done.42, bf16[1536,1152]{1,0:T(8,128)(2,1)S(1)} %copy-done.5, bf16[2048,1536]{1,0:T(8,128)(2,1)} %collective-permute-done.24), kind=kOutput, calls=%fused_computation.30 | convolution fusion | flops 1814298624 | bytes 7864320 | tf_op jit(solution)/shard_map/tf,df->td/dot_general | solution.py:959
  328.6 6.1 %add_convert_fusion = bf16[1024,1536]{1,0:T(8,128)(2,1)S(1)} fusion(bf16[1024,1152]{1,0:T(8,128)(2,1)S(1)} %copy-done.44, bf16[1536,1152]{1,0:T(8,128)(2,1)S(1)} %copy-done.6, bf16[2048,1536]{1,0:T(8,128)(2,1)} %collective-permute-done.24), kind=kOutput, calls=%fused_computation.4 | convolution fusion | flops 3628597248 | bytes 12189696 | tf_op jit(solution)/shard_map/tf,df->td/dot_general | solution.py:959
  334.7 1.5 collective-permute-start.25
  336.6 1.0 multiply_reduce_fusion
  339.4 1.8 collective-permute-start.28
  341.3 40.2 %collective-permute-done.25 = bf16[512,1536]{1,0:T(8,128)(2,1)} collective-permute-done((bf16[512,1536]{1,0:T(8,128)(2,1)}, bf16[512,1536]{1,0:T(8,128)(2,1)}, u32[]{:S(2)}, u32[]{:S(2)}) %collective-permute-start.25) | collective-permute-done | bytes 1572896 | tf_op jit(solution)/shard_map/ppermute | solution.py:24
  381.5 2.9 add_convert_fusion.2
  384.4 4.2 collective-permute-start.31
  388.7 8.6 %collective-permute-done.30 = f32[168,128]{1,0:T(8,128)S(1)} collective-permute-done((f32[168,128]{1,0:T(8,128)S(1)}, f32[168,128]{1,0:T(8,128)S(1)}, u32[]{:S(2)}, u32[]{:S(2)}) %collective-permute-start.30) | collective-permute-done | bytes 86048 | tf_op jit(solution)/shard_map/ppermute | solution.py:24
  397.4 6.0 %reduce-scatter.5.cloned.1.call-done = bf16[384,1152]{1,0:T(8,128)(2,1)} async-done(((bf16[1536,1152]{1,0:T(8,128)(2,1)}), bf16[384,1152]{1,0:T(8,128)(2,1)}) %reduce-scatter.5.cloned.1.call-update) | async-done | bytes 884752 | tf_op jit(solution)/shard_map/reduce_scatter | solution.py:970
  403.4 4.7 collective-permute-start.32
  408.1 3.1 add_bitcast_fusion.1
  411.5 1.7 collective-permute-start.36
  413.3 18.0 %collective-permute-done.32 = bf16[256,1536]{1,0:T(8,128)(2,1)S(1)} collective-permute-done((bf16[256,1536]{1,0:T(8,128)(2,1)S(1)}, bf16[256,1536]{1,0:T(8,128)(2,1)S(1)}, u32[]{:S(2)}, u32[]{:S(2)}) %collective-permute-start.32) | collective-permute-done | bytes 786464 | tf_op jit(solution)/shard_map/ppermute | solution.py:24
  431.2 1.9 convert_add_fusion.2
  433.8 4.4 collective-permute-done.34
  438.3 9.1 %collective-permute-start.35 = (f32[168,128]{1,0:T(8,128)S(1)}, f32[168,128]{1,0:T(8,128)S(1)}, u32[]{:S(2)}, u32[]{:S(2)}) collective-permute-start(f32[168,128]{1,0:T(8,128)S(1)} %add.209), channel_id=1, source_target_pairs={{0,16},{8,24},{16,0},{24,8},{1,17},{9,25},{17,1},{25,9},{2,18},{10... | collective-permute-start | bytes 258056 | tf_op jit(solution)/shard_map/ppermute | solution.py:24
  447.5 3.4 fusion.8
  452.3 1.5 reshape.221
  453.7 1.4 fusion.29
  455.1 1.3 slice_bitcast_fusion.3
  456.4 1.3 slice_bitcast_fusion.2
  457.8 1.6 pad_maximum_fusion.piece_ref
  459.4 6.2 %assemble_out_weight_grad.1 = f32[768,1536]{1,0:T(8,128)} custom-call(s32[1]{0:T(128)} %bitcast.place_ref, bf16[8,96,1536]{2,1,0:T(8,128)(2,1)} %pad_maximum_fusion.piece_ref), custom_call_target="tpu_custom_call" | custom-call | flops 5500000256 | bytes 7077888 | tf_op jit(solution)/shard_map/assemble_out_weight_grad/pallas_call | solution.py:810
  465.6 2.1 all-gather.6.cloned.1.call-done
  467.7 8.2 %assemble_in_weight_grad.1 = f32[6448,384]{1,0:T(8,128)} custom-call(bf16[8,384,1152]{2,1,0:T(8,128)(2,1)} %bitcast.82), custom_call_target="tpu_custom_call" | custom-call | flops 8800000000 | bytes 14856192 | tf_op jit(solution)/shard_map/assemble_in_weight_grad/pallas_call | solution.py:844
  (237 shorter events, 21.2 us)
Async XLA Ops:
  7.2 88.2 %all-gather.4.cloned.1.call-start = ((), (), s32[]{:S(2)}) async-start(), calls=%async_computation.2 | async-start | bytes 4423680 | tf_op jit(solution)/shard_map/all_gather | solution.py:900
  11.8 149.4 %all-reduce.6.cloned.1.call-start = ((), (), s32[]{:S(2)}) async-start(), calls=%async_computation.3 | async-start | bytes 2359296 | tf_op jit(solution)/shard_map/psum | solution.py:192
  14.4 20.5 %collective-permute-start = (bf16[256,1536]{1,0:T(8,128)(2,1)S(1)}, bf16[256,1536]{1,0:T(8,128)(2,1)S(1)}, u32[]{:S(2)}, u32[]{:S(2)}) collective-permute-start(bf16[256,1536]{1,0:T(8,128)(2,1)S(1)} %get-tuple-element.282), channel_id=1, source_target_pairs={{0,2},{1,3},{2,0},{3,1},{4,6},{5,7},{6,4},{7,5},{8,10},{9,11},{10,... | collective-permute-start | bytes 2359304 | tf_op jit(solution)/shard_map/ppermute | solution.py:24
  17.4 19.6 %collective-permute-start.3 = (bf16[256,1536]{1,0:T(8,128)(2,1)S(1)}, bf16[256,1536]{1,0:T(8,128)(2,1)S(1)}, u32[]{:S(2)}, u32[]{:S(2)}) collective-permute-start(bf16[256,1536]{1,0:T(8,128)(2,1)S(1)} %get-tuple-element.281), channel_id=1, source_target_pairs={{0,4},{1,5},{2,6},{3,7},{4,0},{5,1},{6,2},{7,3},{8,12},{9,13},{10,... | collective-permute-start | bytes 2359304 | tf_op jit(solution)/shard_map/ppermute | solution.py:24
  35.1 3.9 collective-permute-start.2
  35.2 36.9 %collective-permute-start.1 = (bf16[512,1536]{1,0:T(8,128)(2,1)S(1)}, bf16[512,1536]{1,0:T(8,128)(2,1)}, u32[]{:S(2)}, u32[]{:S(2)}) collective-permute-start(bf16[512,1536]{1,0:T(8,128)(2,1)S(1)} %pad_maximum_fusion.1.refs_0_), channel_id=1, source_target_pairs={{0,4},{1,5},{2,6},{3,7},{4,0},{5,1},{6,2},{7,3},{8,12},{9,13},{10,... | collective-permute-start | bytes 4718600 | tf_op jit(solution)/shard_map/ppermute | solution.py:24
  37.1 35.0 %copy-start.10 = (bf16[512,1536]{1,0:T(8,128)(2,1)}, bf16[512,1536]{1,0:T(8,128)(2,1)S(1)}, u32[]{:S(2)}) copy-start(bf16[512,1536]{1,0:T(8,128)(2,1)S(1)} %pad_maximum_fusion.2.refs_4_) | copy-start | bytes 4718596
  37.1 39.9 %copy-start.37 = (f32[48]{0:T(128)S(1)}, f32[48]{0:T(128)}, u32[]{:S(2)}) copy-start(f32[48]{0:T(128)} %param.18) | copy-start | bytes 580
  37.1 40.0 %copy-start.28 = (f32[48]{0:T(128)S(1)}, f32[48]{0:T(128)}, u32[]{:S(2)}) copy-start(f32[48]{0:T(128)} %param.17) | copy-start | bytes 580
  37.1 40.0 %copy-start.29 = (f32[48]{0:T(128)S(1)}, f32[48]{0:T(128)}, u32[]{:S(2)}) copy-start(f32[48]{0:T(128)} %param.16) | copy-start | bytes 580
  37.1 40.9 %copy-start.24 = (f32[3328]{0:T(1024)S(1)}, f32[3328]{0:T(1024)}, u32[]{:S(2)}) copy-start(f32[3328]{0:T(1024)} %param.15) | copy-start | bytes 39940
  37.2 41.0 %slice-start.1 = ((f32[3328]{0:T(1024)}), f32[256]{0:T(256)S(1)}, s32[]{:S(2)}) async-start(f32[3328]{0:T(1024)} %param.15), calls=%async_computation.8 | async-start | bytes 2048 | tf_op jit(solution)/shard_map/slice | solution.py:885
  37.2 41.8 %copy-start.20 = (f32[4,3328]{1,0:T(4,128)S(1)}, f32[4,3328]{1,0:T(4,128)}, u32[]{:S(2)}) copy-start(f32[4,3328]{1,0:T(4,128)} %param.14) | copy-start | bytes 159748
  37.2 41.8 %slice-start = ((f32[4,3328]{1,0:T(4,128)}), f32[4,256]{1,0:T(4,128)S(1)}, s32[]{:S(2)}) async-start(f32[4,3328]{1,0:T(4,128)} %param.14), calls=%async_computation.7 | async-start | bytes 8192 | tf_op jit(solution)/shard_map/slice | solution.py:885
  37.2 34.9 %collective-permute-start.5 = (bf16[512,1536]{1,0:T(8,128)(2,1)S(1)}, bf16[512,1536]{1,0:T(8,128)(2,1)S(1)}, u32[]{:S(2)}, u32[]{:S(2)}) collective-permute-start(bf16[512,1536]{1,0:T(8,128)(2,1)S(1)} %pad_maximum_fusion.2.refs_4_), channel_id=1, source_target_pairs={{0,1},{1,0},{2,3},{3,2},{4,5},{5,4},{6,7},{7,6},{8,9},{9,8},{10,11... | collective-permute-start | bytes 4718600 | tf_op jit(solution)/shard_map/ppermute | solution.py:24
  37.4 36.7 %collective-permute-start.4 = (bf16[512,1536]{1,0:T(8,128)(2,1)S(1)}, bf16[512,1536]{1,0:T(8,128)(2,1)}, u32[]{:S(2)}, u32[]{:S(2)}) collective-permute-start(bf16[512,1536]{1,0:T(8,128)(2,1)S(1)} %pad_maximum_fusion.2.refs_4_), channel_id=1, source_target_pairs={{0,2},{1,3},{2,0},{3,1},{4,6},{5,7},{6,4},{7,5},{8,10},{9,11},{10,... | collective-permute-start | bytes 4718600 | tf_op jit(solution)/shard_map/ppermute | solution.py:24
  39.0 35.7 %copy-start.30 = (bf16[512,1536]{1,0:T(8,128)(2,1)}, bf16[512,1536]{1,0:T(8,128)(2,1)S(1)}, u32[]{:S(2)}) copy-start(bf16[512,1536]{1,0:T(8,128)(2,1)S(1)} %collective-permute-done.2.refs_2_) | copy-start | bytes 4718596
  74.2 21.2 %collective-permute-start.6 = (bf16[512,1536]{1,0:T(8,128)(2,1)}, bf16[512,1536]{1,0:T(8,128)(2,1)}, u32[]{:S(2)}, u32[]{:S(2)}) collective-permute-start(bf16[512,1536]{1,0:T(8,128)(2,1)} %collective-permute-done.1.refs_1_), channel_id=1, source_target_pairs={{0,1},{1,0},{2,3},{3,2},{4,5},{5,4},{6,7},{7,6},{8,9},{9,8},{10,11... | collective-permute-start | bytes 4718600 | tf_op jit(solution)/shard_map/ppermute | solution.py:24
  74.2 21.2 %collective-permute-start.7 = (bf16[512,1536]{1,0:T(8,128)(2,1)}, bf16[512,1536]{1,0:T(8,128)(2,1)}, u32[]{:S(2)}, u32[]{:S(2)}) collective-permute-start(bf16[512,1536]{1,0:T(8,128)(2,1)} %collective-permute-done.4.refs_5_), channel_id=1, source_target_pairs={{0,1},{1,0},{2,3},{3,2},{4,5},{5,4},{6,7},{7,6},{8,9},{9,8},{10,11... | collective-permute-start | bytes 4718600 | tf_op jit(solution)/shard_map/ppermute | solution.py:24
  74.7 19.4 %collective-permute-start.8 = (bf16[256,1536]{1,0:T(8,128)(2,1)S(1)}, bf16[256,1536]{1,0:T(8,128)(2,1)S(1)}, u32[]{:S(2)}, u32[]{:S(2)}) collective-permute-start(bf16[256,1536]{1,0:T(8,128)(2,1)S(1)} %get-tuple-element.160), channel_id=1, source_target_pairs={{0,2},{1,3},{2,0},{3,1},{4,6},{5,7},{6,4},{7,5},{8,10},{9,11},{10,... | collective-permute-start | bytes 2359304 | tf_op jit(solution)/shard_map/ppermute | solution.py:24
  76.2 19.2 %collective-permute-start.9 = (bf16[256,1536]{1,0:T(8,128)(2,1)S(1)}, bf16[256,1536]{1,0:T(8,128)(2,1)S(1)}, u32[]{:S(2)}, u32[]{:S(2)}) collective-permute-start(bf16[256,1536]{1,0:T(8,128)(2,1)S(1)} %get-tuple-element.162), channel_id=1, source_target_pairs={{0,4},{1,5},{2,6},{3,7},{4,0},{5,1},{6,2},{7,3},{8,12},{9,13},{10,... | collective-permute-start | bytes 2359304 | tf_op jit(solution)/shard_map/ppermute | solution.py:24
  97.2 64.0 %collective-permute-start.13 = (bf16[512,1536]{1,0:T(8,128)(2,1)}, bf16[512,1536]{1,0:T(8,128)(2,1)}, u32[]{:S(2)}, u32[]{:S(2)}) collective-permute-start(bf16[512,1536]{1,0:T(8,128)(2,1)} %constant_dynamic-update-slice_fusion.2.refs_4_), channel_id=1, source_target_pairs={{0,1},{1,0},{2,3},{3,2},{4,5},{5,4},{6,7},{7,6},{8,9},{9,8},{10,11... | collective-permute-start | bytes 4718600 | tf_op jit(solution)/shard_map/ppermute | solution.py:24
  97.2 64.0 %collective-permute-start.12 = (bf16[512,1536]{1,0:T(8,128)(2,1)}, bf16[512,1536]{1,0:T(8,128)(2,1)}, u32[]{:S(2)}, u32[]{:S(2)}) collective-permute-start(bf16[512,1536]{1,0:T(8,128)(2,1)} %constant_dynamic-update-slice_fusion.2.refs_4_), channel_id=1, source_target_pairs={{0,2},{1,3},{2,0},{3,1},{4,6},{5,7},{6,4},{7,5},{8,10},{9,11},{10,... | collective-permute-start | bytes 4718600 | tf_op jit(solution)/shard_map/ppermute | solution.py:24
  99.7 61.5 %collective-permute-start.11 = (bf16[512,1536]{1,0:T(8,128)(2,1)}, bf16[512,1536]{1,0:T(8,128)(2,1)S(1)}, u32[]{:S(2)}, u32[]{:S(2)}) collective-permute-start(bf16[512,1536]{1,0:T(8,128)(2,1)} %constant_dynamic-update-slice_fusion.refs_0_), channel_id=1, source_target_pairs={{0,1},{1,0},{2,3},{3,2},{4,5},{5,4},{6,7},{7,6},{8,9},{9,8},{10,11... | collective-permute-start | bytes 4718600 | tf_op jit(solution)/shard_map/ppermute | solution.py:24
  100.0 61.3 %collective-permute-start.10 = (bf16[512,1536]{1,0:T(8,128)(2,1)}, bf16[512,1536]{1,0:T(8,128)(2,1)S(1)}, u32[]{:S(2)}, u32[]{:S(2)}) collective-permute-start(bf16[512,1536]{1,0:T(8,128)(2,1)} %constant_dynamic-update-slice_fusion.refs_0_), channel_id=1, source_target_pairs={{0,4},{1,5},{2,6},{3,7},{4,0},{5,1},{6,2},{7,3},{8,12},{9,13},{10,... | collective-permute-start | bytes 4718600 | tf_op jit(solution)/shard_map/ppermute | solution.py:24
  102.3 180.2 %reduce-scatter.3.cloned.1.call-start = ((), (), s32[]{:S(2)}) async-start(), calls=%async_computation.4 | async-start | bytes 1474560 | tf_op jit(solution)/shard_map/reduce_scatter | solution.py:948
  161.3 9.0 %copy-start.32 = (bf16[512,1536]{1,0:T(8,128)(2,1)}, bf16[512,1536]{1,0:T(8,128)(2,1)S(1)}, u32[]{:S(2)}) copy-start(bf16[512,1536]{1,0:T(8,128)(2,1)S(1)} %collective-permute-done.11.refs_2_) | copy-start | bytes 4718596
  161.3 8.9 %collective-permute-start.14 = (bf16[512,1536]{1,0:T(8,128)(2,1)S(1)}, bf16[512,1536]{1,0:T(8,128)(2,1)S(1)}, u32[]{:S(2)}, u32[]{:S(2)}) collective-permute-start(bf16[512,1536]{1,0:T(8,128)(2,1)S(1)} %collective-permute-done.10.refs_1_), channel_id=1, source_target_pairs={{0,1},{1,0},{2,3},{3,2},{4,5},{5,4},{6,7},{7,6},{8,9},{9,8},{10,11... | collective-permute-start | bytes 4718600 | tf_op jit(solution)/shard_map/ppermute | solution.py:24
  161.4 8.9 %collective-permute-start.15 = (bf16[512,1536]{1,0:T(8,128)(2,1)}, bf16[512,1536]{1,0:T(8,128)(2,1)S(1)}, u32[]{:S(2)}, u32[]{:S(2)}) collective-permute-start(bf16[512,1536]{1,0:T(8,128)(2,1)} %collective-permute-done.12.refs_5_), channel_id=1, source_target_pairs={{0,1},{1,0},{2,3},{3,2},{4,5},{5,4},{6,7},{7,6},{8,9},{9,8},{10,11... | collective-permute-start | bytes 4718600 | tf_op jit(solution)/shard_map/ppermute | solution.py:24
  170.3 23.2 %collective-permute-start.17 = (bf16[2048,1536]{1,0:T(8,128)(2,1)}, bf16[2048,1536]{1,0:T(8,128)(2,1)}, u32[]{:S(2)}, u32[]{:S(2)}) collective-permute-start(bf16[2048,1536]{1,0:T(8,128)(2,1)} %convolution_convert_fusion.2), channel_id=1, source_target_pairs={{0,1},{1,0},{2,3},{3,2},{4,5},{5,4},{6,7},{7,6},{8,9},{9,8},{10,11... | collective-permute-start | bytes 18874376 | tf_op jit(solution)/shard_map/ppermute | solution.py:24
  172.8 20.7 %copy-start.36 = (bf16[384,1536]{1,0:T(8,128)(2,1)S(1)}, bf16[384,1536]{1,0:T(8,128)(2,1)}, u32[]{:S(2)}) copy-start(bf16[384,1536]{1,0:T(8,128)(2,1)} %all-reduce.6.cloned.1.call-done.refs_9_) | copy-start | bytes 3538948
  172.8 20.7 %copy-start.39 = (bf16[512,384]{1,0:T(8,128)(2,1)S(1)}, bf16[512,384]{1,0:T(8,128)(2,1)}, u32[]{:S(2)}) copy-start(bf16[512,384]{1,0:T(8,128)(2,1)} %get-tuple-element.185) | copy-start | bytes 1179652
  192.2 1.3 collective-permute-start.16
  193.5 19.3 %slice-start.2 = ((s8[12582912]{0:T(1024)(128)(4,1)}), s8[4194304]{0:T(1024)(128)(4,1)S(1)}, s32[]{:S(2)}) async-start(s8[12582912]{0:T(1024)(128)(4,1)} %bitcast.84), calls=%async_computation.9 | async-start | bytes 8388608
  197.2 15.6 %slice-start.3 = ((s8[12582912]{0:T(1024)(128)(4,1)}), s8[4194304]{0:T(1024)(128)(4,1)S(1)}, s32[]{:S(2)}) async-start(s8[12582912]{0:T(1024)(128)(4,1)} %bitcast.84), calls=%async_computation.10 | async-start | bytes 8388608
  201.0 3.9 collective-permute-start.18
  204.9 7.1 %collective-permute-start.19 = (f32[2,4096]{1,0:T(2,128)S(1)}, f32[2,4096]{1,0:T(2,128)S(1)}, u32[]{:S(2)}, u32[]{:S(2)}) collective-permute-start(f32[2,4096]{1,0:T(2,128)S(1)} %add.183), channel_id=1, source_target_pairs={{0,4},{1,5},{2,6},{3,7},{4,0},{5,1},{6,2},{7,3},{8,12},{9,13},{10,... | collective-permute-start | bytes 98312 | tf_op jit(solution)/shard_map/ppermute | solution.py:24
  219.2 184.2 %reduce-scatter.5.cloned.1.call-start = ((), (), s32[]{:S(2)}) async-start(), calls=%async_computation.5 | async-start | bytes 4423680 | tf_op jit(solution)/shard_map/reduce_scatter | solution.py:970
  219.2 59.7 %collective-permute-start.20 = (bf16[512,1536]{1,0:T(8,128)(2,1)}, bf16[512,1536]{1,0:T(8,128)(2,1)}, u32[]{:S(2)}, u32[]{:S(2)}) collective-permute-start(bf16[512,1536]{1,0:T(8,128)(2,1)} %fusion.15), channel_id=1, source_target_pairs={{0,2},{1,3},{2,0},{3,1},{4,6},{5,7},{6,4},{7,5},{8,10},{9,11},{10,... | collective-permute-start | bytes 4718600 | tf_op jit(solution)/shard_map/ppermute | solution.py:24
  220.8 58.1 %collective-permute-start.21 = (bf16[512,1536]{1,0:T(8,128)(2,1)}, bf16[512,1536]{1,0:T(8,128)(2,1)}, u32[]{:S(2)}, u32[]{:S(2)}) collective-permute-start(bf16[512,1536]{1,0:T(8,128)(2,1)} %fusion.16), channel_id=1, source_target_pairs={{0,4},{1,5},{2,6},{3,7},{4,0},{5,1},{6,2},{7,3},{8,12},{9,13},{10,... | collective-permute-start | bytes 4718600 | tf_op jit(solution)/shard_map/ppermute | solution.py:24
  282.4 14.6 %copy-start.43 = (bf16[4096,1152]{1,0:T(8,128)(2,1)S(1)}, bf16[4096,1152]{1,0:T(8,128)(2,1)}, u32[]{:S(2)}) copy-start(bf16[4096,1152]{1,0:T(8,128)(2,1)} %get-tuple-element.216) | copy-start | bytes 28311556
  295.2 22.8 %collective-permute-start.24 = (bf16[2048,1536]{1,0:T(8,128)(2,1)}, bf16[2048,1536]{1,0:T(8,128)(2,1)}, u32[]{:S(2)}, u32[]{:S(2)}) collective-permute-start(bf16[2048,1536]{1,0:T(8,128)(2,1)} %convolution_convert_fusion.1), channel_id=1, source_target_pairs={{0,1},{1,0},{2,3},{3,2},{4,5},{5,4},{6,7},{7,6},{8,9},{9,8},{10,11... | collective-permute-start | bytes 18874376 | tf_op jit(solution)/shard_map/ppermute | solution.py:24
  295.2 22.5 %collective-permute-start.22 = (bf16[256,1536]{1,0:T(8,128)(2,1)}, bf16[256,1536]{1,0:T(8,128)(2,1)}, u32[]{:S(2)}, u32[]{:S(2)}) collective-permute-start(bf16[256,1536]{1,0:T(8,128)(2,1)} %get-tuple-element.221), channel_id=1, source_target_pairs={{0,4},{1,5},{2,6},{3,7},{4,0},{5,1},{6,2},{7,3},{8,12},{9,13},{10,... | collective-permute-start | bytes 2359304 | tf_op jit(solution)/shard_map/ppermute | solution.py:24
  296.6 21.1 %collective-permute-start.23 = (bf16[256,1536]{1,0:T(8,128)(2,1)}, bf16[256,1536]{1,0:T(8,128)(2,1)}, u32[]{:S(2)}, u32[]{:S(2)}) collective-permute-start(bf16[256,1536]{1,0:T(8,128)(2,1)} %get-tuple-element.223), channel_id=1, source_target_pairs={{0,2},{1,3},{2,0},{3,1},{4,6},{5,7},{6,4},{7,5},{8,10},{9,11},{10,... | collective-permute-start | bytes 2359304 | tf_op jit(solution)/shard_map/ppermute | solution.py:24
  317.7 150.0 %all-gather.6.cloned.1.call-start = ((), (), s32[]{:S(2)}) async-start(), calls=%async_computation.6 | async-start | bytes 7962624 | tf_op jit(solution)/shard_map/all_gather | solution.py:1013
  334.6 46.9 %copy-start.7 = (bf16[1024,1536]{1,0:T(8,128)(2,1)}, bf16[1024,1536]{1,0:T(8,128)(2,1)S(1)}, u32[]{:S(2)}) copy-start(bf16[1024,1536]{1,0:T(8,128)(2,1)S(1)} %add_convert_fusion) | copy-start | bytes 9437188
  334.7 46.8 %collective-permute-start.25 = (bf16[512,1536]{1,0:T(8,128)(2,1)}, bf16[512,1536]{1,0:T(8,128)(2,1)}, u32[]{:S(2)}, u32[]{:S(2)}) collective-permute-start(bf16[512,1536]{1,0:T(8,128)(2,1)} %fusion.13), channel_id=1, source_target_pairs={{0,2},{1,3},{2,0},{3,1},{4,6},{5,7},{6,4},{7,5},{8,10},{9,11},{10,... | collective-permute-start | bytes 4718600 | tf_op jit(solution)/shard_map/ppermute | solution.py:24
  336.2 45.4 %collective-permute-start.26 = (bf16[512,1536]{1,0:T(8,128)(2,1)}, bf16[512,1536]{1,0:T(8,128)(2,1)}, u32[]{:S(2)}, u32[]{:S(2)}) collective-permute-start(bf16[512,1536]{1,0:T(8,128)(2,1)} %fusion.14), channel_id=1, source_target_pairs={{0,4},{1,5},{2,6},{3,7},{4,0},{5,1},{6,2},{7,3},{8,12},{9,13},{10,... | collective-permute-start | bytes 4718600 | tf_op jit(solution)/shard_map/ppermute | solution.py:24
  339.3 1.9 collective-permute-start.27
  339.4 45.0 %collective-permute-start.28 = (bf16[96,1536]{1,0:T(8,128)(2,1)}, bf16[96,1536]{1,0:T(8,128)(2,1)S(1)}, u32[]{:S(2)}, u32[]{:S(2)}) collective-permute-start(bf16[96,1536]{1,0:T(8,128)(2,1)} %reduce-scatter.3.cloned.1.call-done), channel_id=1, source_target_pairs={{0,0},{1,1},{8,2},{9,3},{16,4},{17,5},{24,6},{25,7},{2,8},{3,9},{1... | collective-permute-start | bytes 884744 | tf_op jit(solution)/shard_map/ppermute | solution.py:196
  384.4 19.0 %copy-start.11 = (bf16[256,1536]{1,0:T(8,128)(2,1)S(1)}, bf16[256,1536]{1,0:T(8,128)(2,1)}, u32[]{:S(2)}) copy-start(bf16[256,1536]{1,0:T(8,128)(2,1)} %get-tuple-element.261) | copy-start | bytes 2359300
  384.4 19.0 %collective-permute-start.29 = (bf16[256,1536]{1,0:T(8,128)(2,1)}, bf16[256,1536]{1,0:T(8,128)(2,1)S(1)}, u32[]{:S(2)}, u32[]{:S(2)}) collective-permute-start(bf16[256,1536]{1,0:T(8,128)(2,1)} %get-tuple-element.256), channel_id=1, source_target_pairs={{0,4},{1,5},{2,6},{3,7},{4,0},{5,1},{6,2},{7,3},{8,12},{9,13},{10,... | collective-permute-start | bytes 2359304 | tf_op jit(solution)/shard_map/ppermute | solution.py:24
  384.4 12.9 %collective-permute-start.31 = (bf16[1,96,1536]{2,1,0:T(8,128)(2,1)S(1)}, bf16[1,96,1536]{2,1,0:T(8,128)(2,1)S(1)}, u32[]{:S(2)}, u32[]{:S(2)}) collective-permute-start(bf16[1,96,1536]{2,1,0:T(8,128)(2,1)S(1)} %bitcast.73), channel_id=1, source_target_pairs={{0,2},{1,3},{2,0},{3,1},{4,6},{5,7},{6,4},{7,5},{8,10},{9,11},{10,... | collective-permute-start | bytes 884744 | tf_op jit(solution)/shard_map/ppermute | solution.py:24
  388.7 8.7 %collective-permute-start.30 = (f32[168,128]{1,0:T(8,128)S(1)}, f32[168,128]{1,0:T(8,128)S(1)}, u32[]{:S(2)}, u32[]{:S(2)}) collective-permute-start(f32[168,128]{1,0:T(8,128)S(1)} %fusion.25), channel_id=1, source_target_pairs={{0,2},{1,3},{2,0},{3,1},{4,6},{5,7},{6,4},{7,5},{8,10},{9,11},{10,... | collective-permute-start | bytes 258056 | tf_op jit(solution)/shard_map/ppermute | solution.py:24
  403.4 27.8 %collective-permute-start.32 = (bf16[256,1536]{1,0:T(8,128)(2,1)S(1)}, bf16[256,1536]{1,0:T(8,128)(2,1)S(1)}, u32[]{:S(2)}, u32[]{:S(2)}) collective-permute-start(bf16[256,1536]{1,0:T(8,128)(2,1)S(1)} %copy-done.11), channel_id=1, source_target_pairs={{0,2},{1,3},{2,0},{3,1},{4,6},{5,7},{6,4},{7,5},{8,10},{9,11},{10,... | collective-permute-start | bytes 2359304 | tf_op jit(solution)/shard_map/ppermute | solution.py:24
  408.1 23.1 %copy-start.8 = (bf16[1024,1536]{1,0:T(8,128)(2,1)S(1)}, bf16[1024,1536]{1,0:T(8,128)(2,1)}, u32[]{:S(2)}) copy-start(bf16[1024,1536]{1,0:T(8,128)(2,1)} %copy-done.7) | copy-start | bytes 9437188
  411.2 22.0 %copy-start.1 = (bf16[1,512,1536]{2,1,0:T(8,128)(2,1)S(1)}, bf16[1,512,1536]{2,1,0:T(8,128)(2,1)}, u32[]{:S(2)}) copy-start(bf16[1,512,1536]{2,1,0:T(8,128)(2,1)} %param.11) | copy-start | bytes 4718596
  411.2 22.5 %collective-permute-start.33 = (f32[168,128]{1,0:T(8,128)S(1)}, f32[168,128]{1,0:T(8,128)S(1)}, u32[]{:S(2)}, u32[]{:S(2)}) collective-permute-start(f32[168,128]{1,0:T(8,128)S(1)} %add.202), channel_id=1, source_target_pairs={{0,4},{1,5},{2,6},{3,7},{4,0},{5,1},{6,2},{7,3},{8,12},{9,13},{10,... | collective-permute-start | bytes 258056 | tf_op jit(solution)/shard_map/ppermute | solution.py:24
  411.5 35.8 %collective-permute-start.36 = (bf16[2,96,1536]{2,1,0:T(8,128)(2,1)S(1)}, bf16[2,96,1536]{2,1,0:T(8,128)(2,1)S(1)}, u32[]{:S(2)}, u32[]{:S(2)}) collective-permute-start(bf16[2,96,1536]{2,1,0:T(8,128)(2,1)S(1)} %pad_maximum_fusion.4), channel_id=1, source_target_pairs={{0,4},{1,5},{2,6},{3,7},{4,0},{5,1},{6,2},{7,3},{8,12},{9,13},{10,... | collective-permute-start | bytes 1769480 | tf_op jit(solution)/shard_map/ppermute | solution.py:24
  433.7 13.9 %copy-start.4 = (bf16[1,512,1536]{2,1,0:T(8,128)(2,1)S(1)}, bf16[1,512,1536]{2,1,0:T(8,128)(2,1)}, u32[]{:S(2)}) copy-start(bf16[1,512,1536]{2,1,0:T(8,128)(2,1)} %param.21) | copy-start | bytes 4718596
  433.7 13.9 %copy-start.19 = (f32[512]{0:T(512)S(1)}, f32[512]{0:T(512)}, u32[]{:S(2)}) copy-start(f32[512]{0:T(512)} %copy-done.18) | copy-start | bytes 6148
  433.7 4.6 collective-permute-start.34
  438.3 12.7 %collective-permute-start.35 = (f32[168,128]{1,0:T(8,128)S(1)}, f32[168,128]{1,0:T(8,128)S(1)}, u32[]{:S(2)}, u32[]{:S(2)}) collective-permute-start(f32[168,128]{1,0:T(8,128)S(1)} %add.209), channel_id=1, source_target_pairs={{0,16},{8,24},{16,0},{24,8},{1,17},{9,25},{17,1},{25,9},{2,18},{10... | collective-permute-start | bytes 258056 | tf_op jit(solution)/shard_map/ppermute | solution.py:24
  447.4 10.3 %collective-permute-start.37 = (bf16[4,96,1536]{2,1,0:T(8,128)(2,1)S(1)}, bf16[4,96,1536]{2,1,0:T(8,128)(2,1)S(1)}, u32[]{:S(2)}, u32[]{:S(2)}) collective-permute-start(bf16[4,96,1536]{2,1,0:T(8,128)(2,1)S(1)} %pad_maximum_fusion.3), channel_id=1, source_target_pairs={{0,1},{1,0},{2,3},{3,2},{4,5},{5,4},{6,7},{7,6},{8,9},{9,8},{10,11... | collective-permute-start | bytes 3538952 | tf_op jit(solution)/shard_map/ppermute | solution.py:24
  (29 other events, 109.7 us)
Sparse Core Ops, SparseCore 0:
  12.0 72.6 all-gather.3
  102.4 56.7 all-reduce.5
  219.3 29.6 reduce-scatter.2
  317.8 85.5 reduce-scatter.4
  405.1 62.5 all-gather.5
